TPU v7x, 256 devices: a whole 4x4x8 slice. The times are simulated.
256 devices in a mesh: layer: 2 (over y_lo), row: 4 (over y_hi, core), col: 32 (over z, x).
Axes of the slice: x: 4, y: 4 (y_hi: 2, y_lo: 2; y = y_hi * 2 + y_lo), z: 8, core: 2. Of those that a mesh axis runs over, the one named last changes fastest.
Arguments:
- jac_values: bfloat16 [524288, 768], P(('layer', 'row', 'col')), may hold values from -0.046875 to 0.046875
- row_weights: bfloat16 [524288], P(('layer', 'row', 'col')), may hold values from 1 to 10
- block_cols: int32 [4096, 6], P(('layer', 'row', 'col')), may hold values from 0 to 127, as said below
Outputs:
- gain_band: float32 [16384, 1024], P(('layer', 'col'), 'row')
Inputs may be any that keep to these rules, and one draw needn't show every extreme that they name: Row m of block_cols belongs to the device with linear index d = m // 16 in the order layer, row, col. With h = (d // 128) * 32 + d % 32, its 6 entries are distinct values ((2 * h + k) mod 128) with 0 <= k < 8.
All inputs are finite; a program needn't handle non-finite values.
Results may differ from a plain program's by a relative error of at most 0.0005.
Values sent between devices are 32-bit elements; how exact they have to be, the bound alone decides.
No kernel may reach another device: no remote copies, remote signals or barrier semaphores. Data moves between devices by JAX's collectives and lax.ppermute only.
A program may use at most 64 MiB of HBM per device.

v0:
```python
import jax
import jax.numpy as jnp
from jax import lax
from jax.sharding import PartitionSpec as P

BLOCK = 128
SPAN = 8
BC_DEV = 2


def shifted(value, axis, steps):
    count = lax.axis_size(axis)
    pairs = [(source, (source + steps) % count) for source in range(count)]
    return lax.ppermute(value, axis, pairs)


def band_matrix(values, slot_cols, first_block, total_blocks):
    blocks = slot_cols.shape[0]
    slot_total = slot_cols.shape[1]
    offsets = jnp.mod(slot_cols - first_block, total_blocks)
    select = (offsets[:, :, None] == jnp.arange(SPAN, dtype=jnp.int32)[None, None, :]).astype(
        jnp.bfloat16
    )
    pieces = values.reshape(blocks, BLOCK, slot_total, BLOCK)
    banded = jnp.einsum("bmkc,bks->bmsc", pieces, select, preferred_element_type=jnp.float32)
    return banded.astype(jnp.bfloat16).reshape(blocks * BLOCK, SPAN * BLOCK)


def split_parts(product, home_count):
    tiles = product.reshape(SPAN, BLOCK, SPAN, BLOCK)
    zero_tile = jnp.zeros((BLOCK, BLOCK), jnp.float32)
    parts = []
    for distance in range(home_count):
        by_offset = []
        for offset in range(SPAN):
            rows_here = []
            for within in range(BC_DEV):
                source = BC_DEV * distance + within
                target = source + offset
                rows_here.append(tiles[source, :, target, :] if target < SPAN else zero_tile)
            by_offset.append(jnp.concatenate(rows_here, axis=0))
        parts.append(jnp.stack(by_offset, axis=0))
    return jnp.stack(parts, axis=0)


def route(parts):
    home_count = parts.shape[0]
    running = parts[0]
    for distance in range(1, home_count):
        running = running + shifted(parts[distance], ("layer", "col"), distance)
    return running


def local(jac_values, row_weights, block_cols):
    layer_total = lax.axis_size("layer")
    col_total = lax.axis_size("col")
    home_index = lax.axis_index("layer") * col_total + lax.axis_index("col")
    total_blocks = BC_DEV * layer_total * col_total
    first_block = BC_DEV * home_index
    banded = band_matrix(jac_values, block_cols, first_block, total_blocks)
    weighted = (row_weights.astype(jnp.float32)[:, None] * banded.astype(jnp.float32)).astype(
        jnp.bfloat16
    )
    product = lax.dot_general(
        banded, weighted, (((0,), (0,)), ((), ())), preferred_element_type=jnp.float32
    )
    parts = split_parts(product, SPAN // BC_DEV)
    arrived = route(parts)
    owned = lax.psum_scatter(arrived, "row", scatter_dimension=0, tiled=True)
    return owned.transpose(1, 0, 2).reshape(owned.shape[1], owned.shape[0] * owned.shape[2])


def solution(mesh):
    in_specs = (
        P(("layer", "row", "col"), None),
        P(("layer", "row", "col")),
        P(("layer", "row", "col"), None),
    )
    out_specs = P(("layer", "col"), "row")
    return jax.shard_map(local, mesh=mesh, in_specs=in_specs, out_specs=out_specs, check_vma=False)
```

profile of v0, /device:TPU:1, one launch (start us, length us, event | category | flops | bytes accessed | tf_op | source)
XLA Modules:
  0.0 219.2 jit_solution(15743111194687186216)
XLA Ops:
  6.5 0.0 copy-start
  6.5 0.0 reduce-scatter.2.cloned.1.call-start
  6.5 0.7 add_select_fusion
  7.2 0.1 copy.7
  7.3 7.7 %reshape.20 = bf16[16,128,6,128]{3,2,1,0:T(8,128)(2,1)} reshape(bf16[2048,768]{1,0:T(8,128)(2,1)} %param.3) | data formatting | bytes 6291456 | tf_op jit(solution)/shard_map/reshape | solution.py:24
  15.0 0.0 copy-done
  15.0 3.4 %convolution_convert_fusion = bf16[16,8,128,128]{3,1,2,0:T(8,128)(2,1)S(1)} fusion(bf16[16,128,6,128]{3,2,1,0:T(8,128)(2,1)} %reshape.20, s32[16,6]{1,0:T(8,128)S(1)} %copy.7), kind=kOutput, calls=%fused_computation.3 | convolution fusion | flops 27263744 | bytes 7340416 | tf_op jit(solution)/shard_map/bmkc,bks->bmsc/dot_general | solution.py:25
  18.4 3.0 %copy.20 = bf16[256,8,8,128]{3,1,2,0:T(8,128)(2,1)} copy(bf16[256,8,8,128]{3,2,1,0:T(8,128)(2,1)S(1)} %bitcast.172) | data formatting | bytes 8388608
  21.4 2.4 %fusion = bf16[1024,2048]{0,1:T(8,128)(2,1)} fusion(f32[2048]{0:T(1024)S(1)} %convert_element_type.18, bf16[256,8,8,128]{3,2,1,0:T(8,128)(2,1)S(1)} %bitcast.173), kind=kLoop, calls=%fused_computation.1 | loop fusion | flops 6291456 | bytes 8396800 | tf_op jit(solution)/shard_map/dot_general | solution.py:64
  23.8 6.5 %copy.11 = bf16[1024,2048]{1,0:T(8,128)(2,1)} copy(bf16[1024,2048]{0,1:T(8,128)(2,1)} %fusion) | data formatting | bytes 8388608 | tf_op jit(solution)/shard_map/dot_general | solution.py:64
  30.3 6.5 %copy.10 = bf16[1024,2048]{1,0:T(8,128)(2,1)} copy(bf16[1024,2048]{0,1:T(8,128)(2,1)} %bitcast.174) | data formatting | bytes 8388608 | tf_op jit(solution)/shard_map/dot_general | solution.py:64
  36.8 7.6 %fusion.20 = f32[8,128,8,128]{3,1,2,0:T(8,128)S(1)} fusion(bf16[8,128,2048,1]{2,1,3,0:T(8,128)(2,1)} %bitcast.176, bf16[8,128,2048,1]{2,1,0,3:T(8,128)(2,1)} %bitcast.175), kind=kOutput, calls=%fused_computation.86 | convolution fusion | flops 4294967296 | bytes 12582912 | tf_op jit(solution)/shard_map/dot_general | solution.py:64
  44.4 0.1 slice_bitcast_fusion.20
  44.5 0.1 slice_bitcast_fusion.10
  44.7 2.1 collective-permute-start
  47.0 2.5 %collective-permute-start.1 = (f32[8,256,128]{2,1,0:T(8,128)S(1)}, f32[8,256,128]{2,1,0:T(8,128)S(1)}, u32[]{:S(2)}, u32[]{:S(2)}) collective-permute-start(f32[8,256,128]{2,1,0:T(8,128)S(1)} %broadcast_dynamic-update-slice_fusion), channel_id=1, source_target_pairs={{0,2},{1,3},{2,4},{3,5},{4,6},{5,7},{6,8},{7,9},{8,10},{9,11},{10,... | collective-permute-start | bytes 3145736 | tf_op jit(solution)/shard_map/ppermute | solution.py:14
  49.6 0.1 pad_maximum_fusion
  49.7 2.6 %collective-permute-start.2 = (f32[8,256,128]{2,1,0:T(8,128)S(1)}, f32[8,256,128]{2,1,0:T(8,128)S(1)}, u32[]{:S(2)}, u32[]{:S(2)}) collective-permute-start(f32[8,256,128]{2,1,0:T(8,128)S(1)} %pad_maximum_fusion), channel_id=1, source_target_pairs={{0,3},{1,4},{2,5},{3,6},{4,7},{5,8},{6,9},{7,10},{8,11},{9,12},{10... | collective-permute-start | bytes 3145736 | tf_op jit(solution)/shard_map/ppermute | solution.py:14
  52.4 66.3 %collective-permute-done = f32[8,256,128]{2,1,0:T(8,128)S(1)} collective-permute-done((f32[8,256,128]{2,1,0:T(8,128)S(1)}, f32[8,256,128]{2,1,0:T(8,128)S(1)}, u32[]{:S(2)}, u32[]{:S(2)}) %collective-permute-start) | collective-permute-done | bytes 1048608 | tf_op jit(solution)/shard_map/ppermute | solution.py:14
  118.6 3.0 %collective-permute-done.1 = f32[8,256,128]{2,1,0:T(8,128)S(1)} collective-permute-done((f32[8,256,128]{2,1,0:T(8,128)S(1)}, f32[8,256,128]{2,1,0:T(8,128)S(1)}, u32[]{:S(2)}, u32[]{:S(2)}) %collective-permute-start.1) | collective-permute-done | bytes 1048608 | tf_op jit(solution)/shard_map/ppermute | solution.py:14
  121.6 0.0 collective-permute-done.2
  121.6 1.2 add_add_fusion
  122.8 0.0 reduce-scatter.2.cloned.1.call-update
  122.8 87.6 %reduce-scatter.2.cloned.1.call-done = f32[2,256,128]{2,1,0:T(8,128)} async-done(((f32[8,256,128]{2,1,0:T(8,128)}), f32[2,256,128]{2,1,0:T(8,128)}) %reduce-scatter.2.cloned.1.call-update) | async-done | bytes 262160 | tf_op jit(solution)/shard_map/reduce_scatter | solution.py:69
  210.5 1.1 copy.12
  211.5 0.8 copy.13
  (23 shorter events, 0.3 us)
Async XLA Ops:
  6.5 8.5 %copy-start = (bf16[2048]{0:T(1024)(128)(2,1)S(1)}, bf16[2048]{0:T(1024)(128)(2,1)}, u32[]{:S(2)}) copy-start(bf16[2048]{0:T(1024)(128)(2,1)} %param.4) | copy-start | bytes 12292
  6.5 203.9 %reduce-scatter.2.cloned.1.call-start = ((), (), s32[]{:S(2)}) async-start(), calls=%async_computation.1 | async-start | bytes 1310720 | tf_op jit(solution)/shard_map/reduce_scatter | solution.py:69
  44.7 73.9 %collective-permute-start = (f32[8,256,128]{2,1,0:T(8,128)S(1)}, f32[8,256,128]{2,1,0:T(8,128)S(1)}, u32[]{:S(2)}, u32[]{:S(2)}) collective-permute-start(f32[8,256,128]{2,1,0:T(8,128)S(1)} %broadcast_dynamic-update-slice_fusion.1), channel_id=1, source_target_pairs={{0,1},{1,2},{2,3},{3,4},{4,5},{5,6},{6,7},{7,8},{8,9},{9,10},{10,1... | collective-permute-start | bytes 3145736 | tf_op jit(solution)/shard_map/ppermute | solution.py:14
  47.0 74.7 %collective-permute-start.1 = (f32[8,256,128]{2,1,0:T(8,128)S(1)}, f32[8,256,128]{2,1,0:T(8,128)S(1)}, u32[]{:S(2)}, u32[]{:S(2)}) collective-permute-start(f32[8,256,128]{2,1,0:T(8,128)S(1)} %broadcast_dynamic-update-slice_fusion), channel_id=1, source_target_pairs={{0,2},{1,3},{2,4},{3,5},{4,6},{5,7},{6,8},{7,9},{8,10},{9,11},{10,... | collective-permute-start | bytes 3145736 | tf_op jit(solution)/shard_map/ppermute | solution.py:14
  49.7 72.0 %collective-permute-start.2 = (f32[8,256,128]{2,1,0:T(8,128)S(1)}, f32[8,256,128]{2,1,0:T(8,128)S(1)}, u32[]{:S(2)}, u32[]{:S(2)}) collective-permute-start(f32[8,256,128]{2,1,0:T(8,128)S(1)} %pad_maximum_fusion), channel_id=1, source_target_pairs={{0,3},{1,4},{2,5},{3,6},{4,7},{5,8},{6,9},{7,10},{8,11},{9,12},{10... | collective-permute-start | bytes 3145736 | tf_op jit(solution)/shard_map/ppermute | solution.py:14
Sparse Core Ops, SparseCore 0:
  122.9 87.4 reduce-scatter.1
where the time goes:
time: 220 us; the launch traced here: 219 us
  waiting for transfers between devices  157 us (71%)
  local copies, waits for them, and re-layouts  26 us (12%)
  between operations  13.6 us (6%)
  matrix products  11 us (5%)
  starting transfers between devices  7.24 us (3%)
  other arithmetic  4.5 us (2%)
    reduce_scatter x1, waiting for transfers between devices, local(): owned = lax.psum_scatter(arrived, 'row', scatter_dimension=0, tiled=True)  87.6 us
    ppermute x3, waiting for transfers between devices, shifted(): return lax.ppermute(value, axis, pairs)  69.3 us
    dot_general x2, local copies, waits for them, and re-layouts, local(): lax.dot_general(banded, weighted, (((0,), (0,)), ((), ())), preferred_ele...  13 us
    reshape x1, local copies, waits for them, and re-layouts, band_matrix(): pieces = values.reshape(blocks, BLOCK, slot_total, BLOCK)  7.66 us
    dot_general x1, matrix products, local(): lax.dot_general(banded, weighted, (((0,), (0,)), ((), ())), preferred_ele...  7.58 us
    ppermute x3, starting transfers between devices, shifted(): return lax.ppermute(value, axis, pairs)  7.24 us
  transfers between devices with their start and end apart: 4, of which 3 were waited for; matrix products, arithmetic and copies ran while one was open for 0% of the time, Pallas kernels for 0%

commit v1 on v0

v1 whole, which is shorter than its diff:
```python
import jax
import jax.numpy as jnp
from jax import lax
from jax.experimental import pallas as pl
from jax.experimental.pallas import tpu as pltpu
from jax.sharding import PartitionSpec as P

BLOCK = 128
SPAN = 8
SLOTS = 6
HOMES = 64
COLS = 32
WINDOW = 128
AXES = ("layer", "row", "col")

CORE_OFFSETS = ((0, 1, 4, 5), (2, 3, 6, 7))


def device_index(home, row):
    return ((home // COLS) * 4 + row) * COLS + home % COLS


def pairs_of(rows, distance):
    return [
        (device_index(home, source), device_index((home + distance) % HOMES, target))
        for source, target in rows
        for home in range(HOMES)
    ]


def slot_tiles(distance, core):
    tiles = []
    for offset in CORE_OFFSETS[core]:
        for within in range(2):
            source = 2 * distance + within
            tiles.append((source + offset, source) if source + offset < SPAN else None)
    return tiles


def store_tiles(product, first_target, distance, slots, base, core, out_ref):
    for owner in range(2):
        place = jnp.bitwise_xor(core, owner)
        tiles = slot_tiles(distance, owner)
        for slot in range(slots):
            if tiles[slot] is None:
                value = jnp.zeros((BLOCK, BLOCK), jnp.float32)
            else:
                target, source = tiles[slot]
                top = (target - first_target) * BLOCK
                left = (source - 2 * distance) * BLOCK
                value = product[top : top + BLOCK, left : left + BLOCK]
            out_ref[place, base + slot] = value


def transpose_block(h_ref, w_ref, at_ref, block, first, count):
    rows = pl.ds(block * BLOCK, BLOCK)
    weights = w_ref[pl.ds(block, 1), :].astype(jnp.float32)
    for target in range(count):
        tile = h_ref[rows, (first + target) * BLOCK : (first + target + 1) * BLOCK]
        turned = tile.T.astype(jnp.float32) * weights
        at_ref[target * BLOCK : (target + 1) * BLOCK, pl.ds(block * BLOCK, BLOCK)] = turned.astype(jnp.bfloat16)


def far_kernel(cols_ref, w_ref, jac_ref, h_ref, at_ref, out_ref, sems):
    home = lax.axis_index("layer") * COLS + lax.axis_index("col")
    core = lax.axis_index("row") % 2
    blocks = jac_ref.shape[0] // BLOCK

    def fetch(block, carry):
        rows = pl.ds(pl.multiple_of(block * BLOCK, BLOCK), BLOCK)
        h_ref[rows, :] = jnp.zeros((BLOCK, SPAN * BLOCK), jnp.bfloat16)
        for slot in range(SLOTS):
            offset = jnp.bitwise_and(cols_ref[slot, block] - 2 * home, WINDOW - 1)
            pltpu.make_async_copy(
                jac_ref.at[rows, slot * BLOCK : (slot + 1) * BLOCK],
                h_ref.at[rows, pl.ds(pl.multiple_of(offset * BLOCK, BLOCK), BLOCK)],
                sems.at[block],
            ).start()
        return carry

    lax.fori_loop(0, blocks, fetch, 0)

    for block in range(blocks):
        rows = pl.ds(block * BLOCK, BLOCK)
        pltpu.make_async_copy(
            jac_ref.at[rows, :], h_ref.at[rows, 0 : SLOTS * BLOCK], sems.at[block]
        ).wait()
        transpose_block(h_ref, w_ref, at_ref, block, 4, 4)

    product = jnp.dot(at_ref[...], h_ref[:, 512:768], preferred_element_type=jnp.float32)
    store_tiles(product, 4, 2, 4, 0, core, out_ref)
    product = jnp.dot(at_ref[256:, :], h_ref[:, 768:1024], preferred_element_type=jnp.float32)
    store_tiles(product, 6, 3, 3, 4, core, out_ref)


def middle_kernel(w_ref, h_ref, hi_ref, at_ref, out_ref):
    core = lax.axis_index("row") % 2
    for block in range(h_ref.shape[0] // BLOCK):
        transpose_block(h_ref, w_ref, at_ref, block, 2, 2)
    product = jnp.concatenate(
        [
            jnp.dot(at_ref[...], h_ref[:, 256:512], preferred_element_type=jnp.float32),
            jnp.dot(hi_ref[...], h_ref[:, 256:512], preferred_element_type=jnp.float32),
        ],
        axis=0,
    )
    store_tiles(product, 2, 1, 7, 0, core, out_ref)


def near_kernel(w_ref, h_ref, hi_ref, mid_ref, out_ref, at_ref):
    core = lax.axis_index("row") % 2
    for block in range(h_ref.shape[0] // BLOCK):
        transpose_block(h_ref, w_ref, at_ref, block, 0, 2)
    product = jnp.concatenate(
        [
            jnp.dot(at_ref[...], h_ref[:, 0:256], preferred_element_type=jnp.float32),
            jnp.dot(mid_ref[...], h_ref[:, 0:256], preferred_element_type=jnp.float32),
            jnp.dot(hi_ref[...], h_ref[:, 0:256], preferred_element_type=jnp.float32),
        ],
        axis=0,
    )
    store_tiles(product, 0, 0, 8, 0, core, out_ref)


def final_kernel(a_ref, b_ref, c_ref, d_ref, out_ref):
    for pair in range(2):
        for within in range(2):
            slot = 2 * pair + within
            tile = a_ref[slot] + b_ref[slot] + c_ref[slot] + d_ref[slot]
            out_ref[within * BLOCK : (within + 1) * BLOCK, pair * BLOCK : (pair + 1) * BLOCK] = tile.T


VMEM = pl.BlockSpec(memory_space=pltpu.VMEM)
SMEM = pl.BlockSpec(memory_space=pltpu.SMEM)
ANY = pl.BlockSpec(memory_space=pl.ANY)
PARAMS = pltpu.CompilerParams(vmem_limit_bytes=32 * 1024 * 1024)


def bf16(*shape):
    return jax.ShapeDtypeStruct(shape, jnp.bfloat16)


def f32(*shape):
    return jax.ShapeDtypeStruct(shape, jnp.float32)


def cost(rows, read, written):
    return pl.CostEstimate(flops=2 * rows * 256 * 2048, bytes_accessed=read + written, transcendentals=0)


def swap_core(value):
    return lax.ppermute(value, AXES, pairs_of([(0, 1), (1, 0), (2, 3), (3, 2)], 0))


def local(jac_values, row_weights, block_cols):
    rows = jac_values.shape[0]
    upper = lax.axis_index("row") >= 2
    weights = row_weights.reshape(rows // BLOCK, BLOCK)
    h, hi, far = pl.pallas_call(
        far_kernel,
        out_shape=(bf16(rows, 1024), bf16(512, rows), f32(2, 7, BLOCK, BLOCK)),
        in_specs=[SMEM, VMEM, ANY],
        out_specs=(VMEM, VMEM, VMEM),
        scratch_shapes=[pltpu.SemaphoreType.DMA((rows // BLOCK,))],
        compiler_params=PARAMS,
        cost_estimate=cost(768, 3 << 20, 0),
        name="far",
    )(block_cols.T, weights, jac_values)
    far_in = swap_core(far[1])
    mid, middle = pl.pallas_call(
        middle_kernel,
        out_shape=(bf16(256, rows), f32(2, 7, BLOCK, BLOCK)),
        in_specs=[VMEM] * 3,
        out_specs=(VMEM, VMEM),
        compiler_params=PARAMS,
        cost_estimate=cost(768, 0, 0),
        name="middle",
    )(weights, h, hi)
    far_sum = far[0] + far_in
    two = lax.ppermute(far_sum[:4], AXES, pairs_of([(r, r) for r in range(4)], 2))
    three = lax.ppermute(far_sum[4:], AXES, pairs_of([(0, 0), (2, 2)], 3))
    middle_in = swap_core(middle[1])
    near = pl.pallas_call(
        near_kernel,
        out_shape=f32(2, 8, BLOCK, BLOCK),
        in_specs=[VMEM] * 4,
        out_specs=VMEM,
        scratch_shapes=[pltpu.VMEM((256, rows), jnp.bfloat16)],
        compiler_params=PARAMS,
        cost_estimate=cost(1024, 0, 0),
        name="near",
    )(weights, h, hi, mid)
    middle_sum = middle[0] + middle_in
    low, high = middle_sum[:4], jnp.pad(middle_sum[4:], ((0, 1), (0, 0), (0, 0)))
    one_same = lax.ppermute(jnp.where(upper, high, low), AXES, pairs_of([(0, 0), (1, 1), (2, 2)], 1))
    one_cross = lax.ppermute(jnp.where(upper, low, high), AXES, pairs_of([(2, 0), (3, 1), (0, 2)], 1))
    near_in = swap_core(near[1])
    near_sum = near[0] + near_in
    low = near_sum[:4] + two + jnp.pad(three, ((0, 1), (0, 0), (0, 0)))
    high = near_sum[4:]
    crossed = lax.ppermute(jnp.where(upper, low, high), AXES, pairs_of([(0, 2), (1, 3), (2, 0), (3, 1)], 0))
    kept = jnp.where(upper, high, low)
    return pl.pallas_call(
        final_kernel,
        out_shape=f32(256, 256),
        in_specs=[VMEM] * 4,
        out_specs=VMEM,
        compiler_params=PARAMS,
        name="last",
    )(kept, crossed, one_same, one_cross)


def solution(mesh):
    in_specs = (P(AXES, None), P(AXES), P(AXES, None))
    return jax.shard_map(local, mesh=mesh, in_specs=in_specs, out_specs=P(("layer", "col"), "row"), check_vma=False)
```

time: 220 us -> 46.8 us (0.21)
  the two profiles are of different devices: /device:TPU:1 before, /device:TPU:8 now
where the time goes in v1:
time: 46.8 us; the launch traced here: 46.5 us
  starting transfers between devices  18.3 us (39%)
  waiting for transfers between devices  12 us (26%)
  Pallas kernels  8.03 us (17%)
  local copies, waits for them, and re-layouts  5.72 us (12%)
  other arithmetic  2.29 us (5%)
    pallas_call x1, Pallas kernels, local(): pl.pallas_call(far_kernel, out_shape=(bf16(rows, 1024), bf16(512, rows),...  4.69 us
    ppermute x1, starting transfers between devices, local(): three = lax.ppermute(far_sum[4:], AXES, pairs_of([(0, 0), (2, 2)], 3))  4.67 us
    ppermute x1, waiting for transfers between devices, local(): lax.ppermute(jnp.where(upper, low, high), AXES, pairs_of([(0, 2), (1, 3),...  4.53 us
    ppermute x1, starting transfers between devices, local(): lax.ppermute(jnp.where(upper, low, high), AXES, pairs_of([(2, 0), (3, 1),...  4.53 us
    ppermute x1, waiting for transfers between devices, local(): lax.ppermute(jnp.where(upper, low, high), AXES, pairs_of([(2, 0), (3, 1),...  4.02 us
    ppermute x1, starting transfers between devices, local(): lax.ppermute(jnp.where(upper, high, low), AXES, pairs_of([(0, 0), (1, 1),...  3.71 us
    ppermute x1, waiting for transfers between devices, local(): lax.ppermute(far_sum[:4], AXES, pairs_of([(r, r) for r in range(4)], 2))  3.37 us
    unnamed x6, local copies, waits for them, and re-layouts  3.26 us
  transfers between devices with their start and end apart: 8, of which 4 were waited for; matrix products, arithmetic and copies ran while one was open for 9% of the time, Pallas kernels for 5%

profile of v1, /device:TPU:8, one launch (start us, length us, event | category | flops | bytes accessed | tf_op | source)
XLA Modules:
  0.0 46.5 jit_solution(16579686395012662133)
XLA Ops:
  0.0 0.0 copy-start
  0.0 1.9 %copy-done = bf16[2048,768]{1,0:T(8,128)(2,1)S(1)} copy-done((bf16[2048,768]{1,0:T(8,128)(2,1)S(1)}, bf16[2048,768]{1,0:T(8,128)(2,1)}, u32[]{:S(2)}) %copy-start) | copy-done | bytes 3145752
  1.9 0.0 copy-start.1
  1.9 0.7 %copy-done.1 = bf16[2048]{0:T(1024)(128)(2,1)S(1)} copy-done((bf16[2048]{0:T(1024)(128)(2,1)S(1)}, bf16[2048]{0:T(1024)(128)(2,1)}, u32[]{:S(2)}) %copy-start.1) | copy-done | bytes 4120
  2.6 0.0 copy-start.2
  2.6 0.7 %copy-done.2 = s32[16,6]{0,1:T(8,128)S(1)} copy-done((s32[16,6]{0,1:T(8,128)S(1)}, s32[16,6]{0,1:T(8,128)}, u32[]{:S(2)}) %copy-start.2) | copy-done | bytes 408
  3.3 4.7 %far.1 = (bf16[2048,1024]{1,0:T(8,128)(2,1)S(1)}, bf16[512,2048]{1,0:T(8,128)(2,1)S(1)}, f32[2,7,128,128]{3,2,1,0:T(8,128)S(1)}) custom-call(s32[6,16]{1,0:T(8,128)S(1)} %bitcast.19, bf16[16,128]{1,0:T(8,128)(2,1)S(1)} %bitcast.16, bf16[2048,768]{1,0:T(8,128)(2,1)S(1)} %copy-done), custom_call_target="tpu_custom_call" | custom-call | flops 805306368 | bytes 3145728 | tf_op jit(solution)/shard_map/far/pallas_call | solution.py:159
  8.0 0.8 %slice_bitcast_fusion.3 = f32[7,128,128]{2,1,0:T(8,128)} fusion(f32[2,7,128,128]{3,2,1,0:T(8,128)S(1)} %get-tuple-element.13), kind=kLoop, calls=%fused_computation.6 | loop fusion | bytes 917504 | tf_op jit(solution)/shard_map/squeeze | solution.py:169
  8.8 0.0 collective-permute-start.1
  8.8 1.1 %middle.1 = (bf16[256,2048]{1,0:T(8,128)(2,1)S(1)}, f32[2,7,128,128]{3,2,1,0:T(8,128)S(1)}) custom-call(bf16[16,128]{1,0:T(8,128)(2,1)S(1)} %bitcast.17, bf16[2048,1024]{1,0:T(8,128)(2,1)S(1)} %get-tuple-element.10.h_ref, bf16[512,2048]{1,0:T(8,128)(2,1)S(1)} %get-tuple-element.11.hi_ref), custom_call_target="tpu_custom_call" | custom-call | flops 805306368 | tf_op jit(solution)/shard_map/middle/pallas_call | solution.py:170
  9.9 0.8 %slice_bitcast_fusion.2 = f32[7,128,128]{2,1,0:T(8,128)} fusion(f32[2,7,128,128]{3,2,1,0:T(8,128)S(1)} %get-tuple-element.14), kind=kLoop, calls=%fused_computation.5 | loop fusion | bytes 917504 | tf_op jit(solution)/shard_map/squeeze | solution.py:182
  10.7 0.5 %collective-permute-start.5 = (f32[7,128,128]{2,1,0:T(8,128)}, f32[7,128,128]{2,1,0:T(8,128)}, u32[]{:S(2)}, u32[]{:S(2)}) collective-permute-start(f32[7,128,128]{2,1,0:T(8,128)} %slice_bitcast_fusion.2), channel_id=1, source_target_pairs={{0,32},{1,33},{2,34},{3,35},{4,36},{5,37},{6,38},{7,39},{8,40},{9,... | collective-permute-start | bytes 1376264 | tf_op jit(solution)/shard_map/ppermute | solution.py:152
  11.2 1.4 %near.1 = f32[2,8,128,128]{3,2,1,0:T(8,128)S(1)} custom-call(bf16[16,128]{1,0:T(8,128)(2,1)S(1)} %bitcast.18, bf16[2048,1024]{1,0:T(8,128)(2,1)S(1)} %get-tuple-element.10.h_ref, bf16[512,2048]{1,0:T(8,128)(2,1)S(1)} %get-tuple-element.11.hi_ref, bf16[256,2048]{1,0:T(8,128)(2,1)S(1)} %get-tuple-element.12.mid_ref), custom_call_target="tpu_custom_call" | custom-call | flops 1073741824 | tf_op jit(solution)/shard_map/near/pallas_call | solution.py:183
  12.6 0.8 %slice_bitcast_fusion = f32[8,128,128]{2,1,0:T(8,128)} fusion(f32[2,8,128,128]{3,2,1,0:T(8,128)S(1)} %near.1), kind=kLoop, calls=%fused_computation | loop fusion | bytes 1048576 | tf_op jit(solution)/shard_map/squeeze | solution.py:197
  13.4 0.0 collective-permute-start
  13.4 0.0 collective-permute-done.1
  13.4 1.1 %bitcast_add_fusion.1 = f32[7,128,128]{2,1,0:T(8,128)S(1)} fusion(f32[7,128,128]{2,1,0:T(8,128)} %collective-permute-done.1, f32[2,7,128,128]{3,2,1,0:T(8,128)S(1)} %get-tuple-element.13), kind=kLoop, calls=%fused_computation.4 | loop fusion | flops 114688 | bytes 1376256 | tf_op jit(solution)/shard_map/add | solution.py:179
  14.5 4.7 %collective-permute-start.3 = (f32[3,128,128]{2,1,0:T(8,128)S(1)}, f32[3,128,128]{2,1,0:T(8,128)S(1)}, u32[]{:S(2)}, u32[]{:S(2)}) collective-permute-start(f32[3,128,128]{2,1,0:T(8,128)S(1)} %slice.53), channel_id=1, source_target_pairs={{0,3},{1,4},{2,5},{3,6},{4,7},{5,8},{6,9},{7,10},{8,11},{9,12},{10... | collective-permute-start | bytes 589832 | tf_op jit(solution)/shard_map/ppermute | solution.py:181
  19.2 2.2 %collective-permute-start.2 = (f32[4,128,128]{2,1,0:T(8,128)S(1)}, f32[4,128,128]{2,1,0:T(8,128)S(1)}, u32[]{:S(2)}, u32[]{:S(2)}) collective-permute-start(f32[4,128,128]{2,1,0:T(8,128)S(1)} %slice.52), channel_id=1, source_target_pairs={{0,2},{1,3},{2,4},{3,5},{4,6},{5,7},{6,8},{7,9},{8,10},{9,11},{10,... | collective-permute-start | bytes 786440 | tf_op jit(solution)/shard_map/ppermute | solution.py:180
  21.4 0.0 collective-permute-done.5
  21.4 1.1 %bitcast_add_fusion = f32[7,128,128]{2,1,0:T(8,128)S(1)} fusion(f32[7,128,128]{2,1,0:T(8,128)} %collective-permute-done.5, f32[2,7,128,128]{3,2,1,0:T(8,128)S(1)} %get-tuple-element.14), kind=kLoop, calls=%fused_computation.3 | loop fusion | flops 114688 | bytes 1376256 | tf_op jit(solution)/shard_map/add | solution.py:193
  22.6 4.5 %collective-permute-start.7 = (f32[4,128,128]{2,1,0:T(8,128)S(1)}, f32[4,128,128]{2,1,0:T(8,128)S(1)}, u32[]{:S(2)}, u32[]{:S(2)}) collective-permute-start(f32[4,128,128]{2,1,0:T(8,128)S(1)} %get-tuple-element.17), channel_id=1, source_target_pairs={{64,1},{65,2},{66,3},{67,4},{68,5},{69,6},{70,7},{71,8},{72,9},{73... | collective-permute-start | bytes 786440 | tf_op jit(solution)/shard_map/ppermute | solution.py:196
  27.1 3.7 %collective-permute-start.6 = (f32[4,128,128]{2,1,0:T(8,128)S(1)}, f32[4,128,128]{2,1,0:T(8,128)S(1)}, u32[]{:S(2)}, u32[]{:S(2)}) collective-permute-start(f32[4,128,128]{2,1,0:T(8,128)S(1)} %get-tuple-element.18), channel_id=1, source_target_pairs={{0,1},{1,2},{2,3},{3,4},{4,5},{5,6},{6,7},{7,8},{8,9},{9,10},{10,1... | collective-permute-start | bytes 786440 | tf_op jit(solution)/shard_map/ppermute | solution.py:195
  30.8 0.0 collective-permute-done
  30.8 0.1 fusion
  30.9 0.0 collective-permute-done.3
  30.9 3.4 %collective-permute-done.2 = f32[4,128,128]{2,1,0:T(8,128)S(1)} collective-permute-done((f32[4,128,128]{2,1,0:T(8,128)S(1)}, f32[4,128,128]{2,1,0:T(8,128)S(1)}, u32[]{:S(2)}, u32[]{:S(2)}) %collective-permute-start.2) | collective-permute-done | bytes 262176 | tf_op jit(solution)/shard_map/ppermute | solution.py:180
  34.3 0.1 slice_select_fusion
  34.3 2.7 %collective-permute-start.4 = (f32[4,128,128]{2,1,0:T(8,128)S(1)}, f32[4,128,128]{2,1,0:T(8,128)S(1)}, u32[]{:S(2)}, u32[]{:S(2)}) collective-permute-start(f32[4,128,128]{2,1,0:T(8,128)S(1)} %get-tuple-element.15), channel_id=1, source_target_pairs={{0,64},{1,65},{2,66},{3,67},{4,68},{5,69},{6,70},{7,71},{8,72},{9,... | collective-permute-start | bytes 786440 | tf_op jit(solution)/shard_map/ppermute | solution.py:201
  37.0 4.0 %collective-permute-done.7.d_ref = f32[4,128,128]{2,1,0:T(8,128)S(1)} collective-permute-done((f32[4,128,128]{2,1,0:T(8,128)S(1)}, f32[4,128,128]{2,1,0:T(8,128)S(1)}, u32[]{:S(2)}, u32[]{:S(2)}) %collective-permute-start.7) | collective-permute-done | bytes 262176 | tf_op jit(solution)/shard_map/ppermute | solution.py:196
  41.0 0.1 collective-permute-done.6.c_ref
  41.1 4.5 %collective-permute-done.4.b_ref = f32[4,128,128]{2,1,0:T(8,128)S(1)} collective-permute-done((f32[4,128,128]{2,1,0:T(8,128)S(1)}, f32[4,128,128]{2,1,0:T(8,128)S(1)}, u32[]{:S(2)}, u32[]{:S(2)}) %collective-permute-start.4) | collective-permute-done | bytes 262176 | tf_op jit(solution)/shard_map/ppermute | solution.py:201
  45.7 0.8 %last.1 = f32[256,256]{1,0:T(8,128)} custom-call(f32[4,128,128]{2,1,0:T(8,128)S(1)} %get-tuple-element.16.a_ref, f32[4,128,128]{2,1,0:T(8,128)S(1)} %collective-permute-done.4.b_ref, f32[4,128,128]{2,1,0:T(8,128)S(1)} %collective-permute-done.6.c_ref, f32[4,128,128]{2,1,0:T(8,128)S(1)} %collective-permute-done.7.d_ref), custom_call_target="tpu_custom_call" | custom-call | tf_op jit(solution)/shard_map/last/pallas_call | solution.py:203
  (4 shorter events, 0.1 us)
Async XLA Ops:
  0.0 1.9 %copy-start = (bf16[2048,768]{1,0:T(8,128)(2,1)S(1)}, bf16[2048,768]{1,0:T(8,128)(2,1)}, u32[]{:S(2)}) copy-start(bf16[2048,768]{1,0:T(8,128)(2,1)} %jac_ref.1) | copy-start | bytes 9437188
  1.9 0.7 %copy-start.1 = (bf16[2048]{0:T(1024)(128)(2,1)S(1)}, bf16[2048]{0:T(1024)(128)(2,1)}, u32[]{:S(2)}) copy-start(bf16[2048]{0:T(1024)(128)(2,1)} %param.4) | copy-start | bytes 12292
  2.6 0.7 %copy-start.2 = (s32[16,6]{0,1:T(8,128)S(1)}, s32[16,6]{0,1:T(8,128)}, u32[]{:S(2)}) copy-start(s32[16,6]{0,1:T(8,128)} %param.5) | copy-start | bytes 1156
  8.8 4.7 %collective-permute-start.1 = (f32[7,128,128]{2,1,0:T(8,128)}, f32[7,128,128]{2,1,0:T(8,128)}, u32[]{:S(2)}, u32[]{:S(2)}) collective-permute-start(f32[7,128,128]{2,1,0:T(8,128)} %slice_bitcast_fusion.3), channel_id=1, source_target_pairs={{0,32},{1,33},{2,34},{3,35},{4,36},{5,37},{6,38},{7,39},{8,40},{9,... | collective-permute-start | bytes 1376264 | tf_op jit(solution)/shard_map/ppermute | solution.py:152
  10.7 10.8 %collective-permute-start.5 = (f32[7,128,128]{2,1,0:T(8,128)}, f32[7,128,128]{2,1,0:T(8,128)}, u32[]{:S(2)}, u32[]{:S(2)}) collective-permute-start(f32[7,128,128]{2,1,0:T(8,128)} %slice_bitcast_fusion.2), channel_id=1, source_target_pairs={{0,32},{1,33},{2,34},{3,35},{4,36},{5,37},{6,38},{7,39},{8,40},{9,... | collective-permute-start | bytes 1376264 | tf_op jit(solution)/shard_map/ppermute | solution.py:152
  13.4 17.4 %collective-permute-start = (f32[8,128,128]{2,1,0:T(8,128)}, f32[8,128,128]{2,1,0:T(8,128)S(1)}, u32[]{:S(2)}, u32[]{:S(2)}) collective-permute-start(f32[8,128,128]{2,1,0:T(8,128)} %slice_bitcast_fusion), channel_id=1, source_target_pairs={{0,32},{1,33},{2,34},{3,35},{4,36},{5,37},{6,38},{7,39},{8,40},{9,... | collective-permute-start | bytes 1572872 | tf_op jit(solution)/shard_map/ppermute | solution.py:152
  14.5 16.4 %collective-permute-start.3 = (f32[3,128,128]{2,1,0:T(8,128)S(1)}, f32[3,128,128]{2,1,0:T(8,128)S(1)}, u32[]{:S(2)}, u32[]{:S(2)}) collective-permute-start(f32[3,128,128]{2,1,0:T(8,128)S(1)} %slice.53), channel_id=1, source_target_pairs={{0,3},{1,4},{2,5},{3,6},{4,7},{5,8},{6,9},{7,10},{8,11},{9,12},{10... | collective-permute-start | bytes 589832 | tf_op jit(solution)/shard_map/ppermute | solution.py:181
  19.2 15.1 %collective-permute-start.2 = (f32[4,128,128]{2,1,0:T(8,128)S(1)}, f32[4,128,128]{2,1,0:T(8,128)S(1)}, u32[]{:S(2)}, u32[]{:S(2)}) collective-permute-start(f32[4,128,128]{2,1,0:T(8,128)S(1)} %slice.52), channel_id=1, source_target_pairs={{0,2},{1,3},{2,4},{3,5},{4,6},{5,7},{6,8},{7,9},{8,10},{9,11},{10,... | collective-permute-start | bytes 786440 | tf_op jit(solution)/shard_map/ppermute | solution.py:180
  22.6 18.5 %collective-permute-start.7 = (f32[4,128,128]{2,1,0:T(8,128)S(1)}, f32[4,128,128]{2,1,0:T(8,128)S(1)}, u32[]{:S(2)}, u32[]{:S(2)}) collective-permute-start(f32[4,128,128]{2,1,0:T(8,128)S(1)} %get-tuple-element.17), channel_id=1, source_target_pairs={{64,1},{65,2},{66,3},{67,4},{68,5},{69,6},{70,7},{71,8},{72,9},{73... | collective-permute-start | bytes 786440 | tf_op jit(solution)/shard_map/ppermute | solution.py:196
  27.1 14.0 %collective-permute-start.6 = (f32[4,128,128]{2,1,0:T(8,128)S(1)}, f32[4,128,128]{2,1,0:T(8,128)S(1)}, u32[]{:S(2)}, u32[]{:S(2)}) collective-permute-start(f32[4,128,128]{2,1,0:T(8,128)S(1)} %get-tuple-element.18), channel_id=1, source_target_pairs={{0,1},{1,2},{2,3},{3,4},{4,5},{5,6},{6,7},{7,8},{8,9},{9,10},{10,1... | collective-permute-start | bytes 786440 | tf_op jit(solution)/shard_map/ppermute | solution.py:195
  34.3 11.3 %collective-permute-start.4 = (f32[4,128,128]{2,1,0:T(8,128)S(1)}, f32[4,128,128]{2,1,0:T(8,128)S(1)}, u32[]{:S(2)}, u32[]{:S(2)}) collective-permute-start(f32[4,128,128]{2,1,0:T(8,128)S(1)} %get-tuple-element.15), channel_id=1, source_target_pairs={{0,64},{1,65},{2,66},{3,67},{4,68},{5,69},{6,70},{7,71},{8,72},{9,... | collective-permute-start | bytes 786440 | tf_op jit(solution)/shard_map/ppermute | solution.py:201

commit v2 on v0

v2 whole, which is shorter than its diff:
```python
import jax
import jax.numpy as jnp
from jax import lax
from jax.experimental import pallas as pl
from jax.experimental.pallas import tpu as pltpu
from jax.sharding import PartitionSpec as P

BLOCK = 128
SPAN = 8
SLOTS = 6
HOMES = 64
COLS = 32
WINDOW = 128
AXES = ("layer", "row", "col")

def device_index(home, row):
    return ((home // COLS) * 4 + row) * COLS + home % COLS


def pairs_of(rows, distance):
    return [
        (device_index(home, source), device_index((home + distance) % HOMES, target))
        for source, target in rows
        for home in range(HOMES)
    ]


SMALL_PAIRS = pairs_of([(0, 0), (3, 1)], 3) + pairs_of([(1, 2), (2, 3)], 1)
ONE_PAIRS = pairs_of([(0, 0), (3, 1)], 1)
TWO_PAIRS = pairs_of([(1, 1), (2, 0)], 2)
CROSS_PAIRS = pairs_of([(2, 1), (1, 2)], 0)


def tile_at(distance, offset, within):
    source = 2 * distance + within
    return (distance, source, source + offset)


def tiles_of(distance, first_offset, count):
    tiles = [tile_at(distance, first_offset + slot // 2, slot % 2) for slot in range(count)]
    return [tile if tile[2] < SPAN else None for tile in tiles]


LEAD = 8
PAIR = "pair"


def with_pair(distance, count):
    return (distance, [PAIR] + tiles_of(distance, 1, count))


LARGE = (with_pair(1, 6), with_pair(2, 6))
SMALL = (with_pair(3, 1), (None, tiles_of(1, 4, 3)))
NEAR = (with_pair(0, 6), (None, tiles_of(0, 4, 7)))
LARGE_ROWS = LEAD + 7 * BLOCK
TWO_ROWS = LEAD + 6 * BLOCK
SMALL_ROWS = LEAD + 3 * BLOCK
HALF_ROWS = LEAD + 4 * BLOCK
SECOND_HALF = LEAD + 3 * BLOCK


def store_group(products, groups, base, count, first, keep_ref, send_ref):
    row_index = lax.broadcasted_iota(jnp.int32, (BLOCK, BLOCK), 0)
    col_index = lax.broadcasted_iota(jnp.int32, (BLOCK, BLOCK), 1)

    def plain(place):
        distance, source, target = place
        top = (target - 2 * distance) * BLOCK
        left = (source - 2 * distance) * BLOCK
        return products[distance][top : top + BLOCK, left : left + BLOCK]

    def lead_of(group):
        if group[0] is None:
            return jnp.zeros((LEAD, BLOCK), jnp.float32)
        tile = plain(tile_at(group[0], 0, 1))
        diagonal = jnp.sum(jnp.where(row_index == col_index, tile, 0.0), axis=0, keepdims=True)
        return jnp.broadcast_to(diagonal, (LEAD, BLOCK))

    def tile_of(group, slot):
        place = group[1][slot] if slot < len(group[1]) else None
        if place is None:
            return jnp.zeros((BLOCK, BLOCK), jnp.float32)
        if place == PAIR:
            return jnp.where(
                col_index >= row_index, plain(tile_at(group[0], 0, 0)), plain(tile_at(group[0], 0, 1))
            )
        return plain(place)

    def store(rows, zero, one):
        keep_ref[rows, :] = jnp.where(first, zero, one)
        send_ref[rows, :] = jnp.where(first, one, zero)

    store(slice(base, base + LEAD), lead_of(groups[0]), lead_of(groups[1]))
    for slot in range(count):
        top = base + LEAD + slot * BLOCK
        store(slice(top, top + BLOCK), tile_of(groups[0], slot), tile_of(groups[1], slot))


def far_kernel(cols_hbm, w_hbm, jac_ref, h_ref, at_ref, keep_ref, send_ref, stage, cols_ref, w_vmem, sems, side):
    home = lax.axis_index("layer") * COLS + lax.axis_index("col")
    row = lax.axis_index("row")
    first = (row == 0) | (row == 3)
    blocks = jac_ref.shape[0] // BLOCK
    parts = sems.shape[0]
    depth = blocks // parts * BLOCK
    cols_copy = pltpu.make_async_copy(cols_hbm, cols_ref, side.at[0])
    w_copy = pltpu.make_async_copy(w_hbm, w_vmem, side.at[1])
    cols_copy.start()
    w_copy.start()
    copies = []
    for part in range(parts):
        rows = slice(part * depth, (part + 1) * depth)
        copies.append(pltpu.make_async_copy(jac_ref.at[rows, :], stage.at[rows, :], sems.at[part]))
        copies[part].start()
    cols_copy.wait()
    w_copy.wait()
    weights = w_vmem[...].astype(jnp.float32)

    for block in range(blocks):
        if block * BLOCK % depth == 0:
            copies[block * BLOCK // depth].wait()
        rows = slice(block * BLOCK, (block + 1) * BLOCK)
        total, squares = jnp.int32(0), jnp.int32(0)
        for slot in range(SLOTS):
            offset = jnp.bitwise_and(cols_ref[slot, block] - 2 * home, WINDOW - 1)
            total, squares = total + offset, squares + offset * offset
            there = pl.ds(pl.multiple_of(offset * BLOCK, BLOCK), BLOCK)
            tile = stage[rows, slot * BLOCK : (slot + 1) * BLOCK]
            h_ref[rows, there] = tile
            turned = tile.T.astype(jnp.float32) * weights[block : block + 1, :]
            at_ref[there, rows] = turned.astype(jnp.bfloat16)
        total, squares = 28 - total, 140 - squares
        gap_square = 2 * squares - total * total
        gap = jnp.int32(0)
        for step in range(1, SPAN):
            gap = gap + jnp.where(gap_square >= step * step, 1, 0)
        for offset in ((total + gap) >> 1, (total - gap) >> 1):
            there = pl.ds(pl.multiple_of(offset * BLOCK, BLOCK), BLOCK)
            h_ref[rows, there] = jnp.zeros((BLOCK, BLOCK), jnp.bfloat16)
            at_ref[there, rows] = jnp.zeros((BLOCK, BLOCK), jnp.bfloat16)

    products = {
        distance: jnp.dot(
            at_ref[distance * 256 :, :],
            h_ref[:, distance * 256 : (distance + 1) * 256],
            preferred_element_type=jnp.float32,
        )
        for distance in (3, 2, 1)
    }
    store_group(products, LARGE, 0, 7, first, keep_ref, send_ref)
    store_group(products, SMALL, LARGE_ROWS, 3, first, keep_ref, send_ref)


def near_kernel(h_ref, at_ref, keep_ref, send_ref):
    product = jnp.dot(at_ref[...], h_ref[:, 0:256], preferred_element_type=jnp.float32)
    store_group({0: product}, NEAR, 0, 7, lax.axis_index("row") % 2 == 0, keep_ref, send_ref)


def final_kernel(a_ref, b_ref, out_ref, sum_ref):
    row = lax.axis_index("row")
    sum_ref[...] = a_ref[...] + b_ref[...]
    row_index = lax.broadcasted_iota(jnp.int32, (BLOCK, BLOCK), 0)
    col_index = lax.broadcasted_iota(jnp.int32, (BLOCK, BLOCK), 1)

    begin = jnp.where(row == 0, LEAD - BLOCK, jnp.where(row == 1, 0, jnp.where(row == 2, LEAD, BLOCK)))
    paired = sum_ref[LEAD : LEAD + BLOCK, :]
    turned = paired.T
    diagonal = jnp.broadcast_to(sum_ref[0:1, :], (BLOCK, BLOCK))
    symmetric = (
        jnp.where(col_index >= row_index, paired, turned),
        jnp.where(col_index < row_index, paired, jnp.where(col_index > row_index, turned, diagonal)),
    )
    for slot in range(4):
        place = begin + BLOCK * slot
        if slot == 0:
            place = jnp.maximum(place, 0)
        if slot == 3:
            place = jnp.where(row == 3, 0, place)
        tile = sum_ref[pl.ds(pl.multiple_of(place, 8), BLOCK), :].T
        if slot < 2:
            tile = jnp.where(row == 0, symmetric[slot], tile)
        if slot == 3:
            tile = jnp.where(row == 3, 0.0, tile)
        pair, within = slot // 2, slot % 2
        out_ref[within * BLOCK : (within + 1) * BLOCK, pair * BLOCK : (pair + 1) * BLOCK] = tile


VMEM = pl.BlockSpec(memory_space=pltpu.VMEM)
SMEM = pl.BlockSpec(memory_space=pltpu.SMEM)
HBM = pl.BlockSpec(memory_space=pltpu.HBM)
PARAMS = pltpu.CompilerParams(vmem_limit_bytes=16 * 1024 * 1024)


def bf16(*shape):
    return jax.ShapeDtypeStruct(shape, jnp.bfloat16)


def f32(*shape):
    return jax.ShapeDtypeStruct(shape, jnp.float32)


def cost(rows, read, written):
    return pl.CostEstimate(flops=2 * rows * 256 * 2048, bytes_accessed=read + written, transcendentals=0)


def swap_core(value):
    return lax.ppermute(value, AXES, pairs_of([(0, 1), (1, 0), (2, 3), (3, 2)], 0))


def local(jac_values, row_weights, block_cols):
    rows = jac_values.shape[0]
    row = lax.axis_index("row")
    first_core = row % 2 == 0
    owns = (row == 0) | (row == 3)
    far_rows = LARGE_ROWS + SMALL_ROWS
    inputs = (block_cols.T, row_weights.reshape(rows // BLOCK, BLOCK), jac_values)
    h, at, far, far_out = pl.pallas_call(
        far_kernel,
        out_shape=(bf16(rows, 1024), bf16(1024, rows), f32(far_rows, BLOCK), f32(far_rows, BLOCK)),
        in_specs=[HBM] * 3,
        out_specs=(VMEM,) * 4,
        scratch_shapes=[
            pltpu.VMEM(jac_values.shape, jnp.bfloat16),
            pltpu.SMEM((SLOTS, rows // BLOCK), jnp.int32),
            pltpu.VMEM((rows // BLOCK, BLOCK), jnp.bfloat16),
            pltpu.SemaphoreType.DMA((4,)),
            pltpu.SemaphoreType.DMA((2,)),
        ],
        compiler_params=PARAMS,
        cost_estimate=cost(1536, 3 << 20, 0),
        name="far",
    )(*(pltpu.with_memory_space_constraint(value, pltpu.HBM) for value in inputs))
    far_in = swap_core(far_out)
    near, near_out = pl.pallas_call(
        near_kernel,
        out_shape=(f32(LARGE_ROWS, BLOCK), f32(LARGE_ROWS, BLOCK)),
        in_specs=[VMEM] * 2,
        out_specs=(VMEM, VMEM),
        compiler_params=PARAMS,
        cost_estimate=cost(1024, 0, 0),
        name="near",
    )(h, at)
    near_in = swap_core(near_out)
    merged = near + near_in
    crossed = lax.ppermute(merged, AXES, CROSS_PAIRS)
    large = far[:LARGE_ROWS] + far_in[:LARGE_ROWS]
    one = lax.ppermute(large, AXES, ONE_PAIRS)
    two = lax.ppermute(large[:TWO_ROWS], AXES, TWO_PAIRS)
    small = lax.ppermute(far[LARGE_ROWS:] + far_in[LARGE_ROWS:], AXES, SMALL_PAIRS)
    total = jnp.where(owns, merged, 0.0) + one + crossed
    total = total + jnp.pad(two, ((0, LARGE_ROWS - TWO_ROWS), (0, 0)))
    total = total + jnp.pad(small, ((0, LARGE_ROWS - SMALL_ROWS), (0, 0)))
    low = total[:HALF_ROWS]
    high = jnp.pad(total[SECOND_HALF:], ((0, LEAD), (0, 0)))
    kept = jnp.where(first_core, low, high)
    other = swap_core(jnp.where(first_core, high, low))
    return pl.pallas_call(
        final_kernel,
        out_shape=f32(256, 256),
        in_specs=[VMEM] * 2,
        out_specs=VMEM,
        scratch_shapes=[pltpu.VMEM((HALF_ROWS, BLOCK), jnp.float32)],
        compiler_params=PARAMS,
        name="last",
    )(kept, other)


def solution(mesh):
    in_specs = (P(AXES, None), P(AXES), P(AXES, None))
    return jax.shard_map(local, mesh=mesh, in_specs=in_specs, out_specs=P(("layer", "col"), "row"), check_vma=False)
```

time: 220 us -> 40.3 us (0.18)
  waiting for transfers between devices: 157 us -> 16.4 us
  local copies, waits for them, and re-layouts: 26 us -> 0.05 us
  between operations: 13.6 us -> 0.09 us
  matrix products: 11 us -> 0 us
  Pallas kernels: 0 us -> 8.02 us
  starting transfers between devices: 7.24 us -> 15.1 us
  other arithmetic: 4.5 us -> 0.31 us
    reduce_scatter x1 -> x0, waiting for transfers between devices: 87.6 us -> none  [local(): owned = lax.psum_scatter(arrived, 'row', scatter_dimension=0, tiled=True)]
    ppermute x3 -> x7, waiting for transfers between devices: 69.3 us -> 16.4 us  [the longest x1 11.8 us: local(): lax.ppermute(far[LARGE_ROWS:] + far_in[LARGE_ROWS:], AXES, SMALL_PAIRS)]
    dot_general x2 -> x0, local copies, waits for them, and re-layouts: 13 us -> none  [local(): lax.dot_general(banded, weighted, (((0,), (0,)), ((), ())), preferred_ele...]
    dot_general x2 -> x0, matrix products: 11 us -> none  [the longest x1 7.58 us: local(): lax.dot_general(banded, weighted, (((0,), (0,)), ((), ())), preferred_ele...]
    reshape x2 -> x0, local copies, waits for them, and re-layouts: 8.5 us -> none  [the longest x1 7.66 us: band_matrix(): pieces = values.reshape(blocks, BLOCK, slot_total, BLOCK)]
    pallas_call x0 -> x3, Pallas kernels: none -> 8.02 us  [the longest x1 5.87 us: local(): pl.pallas_call(far_kernel, out_shape=(bf16(rows, 1024), bf16(1024, rows),...]
    ppermute x3 -> x7, starting transfers between devices: 7.24 us -> 15.1 us  [the longest x1 4.66 us: local(): two = lax.ppermute(large[:TWO_ROWS], AXES, TWO_PAIRS)]
    unnamed x5 -> x0, local copies, waits for them, and re-layouts: 3.05 us -> none
  transfers between devices with their start and end apart: 4 -> 7, of which waited for: 3 -> 4; matrix products, arithmetic and copies ran while one was open for 0% -> 0% of each run, Pallas kernels for 0% -> 3%
where the time goes in v2:
time: 40.3 us; the launch traced here: 39.9 us
  waiting for transfers between devices  16.4 us (41%)
  starting transfers between devices  15.1 us (37%)
  Pallas kernels  8.02 us (20%)
    ppermute x1, waiting for transfers between devices, local(): lax.ppermute(far[LARGE_ROWS:] + far_in[LARGE_ROWS:], AXES, SMALL_PAIRS)  11.8 us
    pallas_call x1, Pallas kernels, local(): pl.pallas_call(far_kernel, out_shape=(bf16(rows, 1024), bf16(1024, rows),...  5.87 us
    ppermute x1, starting transfers between devices, local(): two = lax.ppermute(large[:TWO_ROWS], AXES, TWO_PAIRS)  4.66 us
    ppermute x3, starting transfers between devices, swap_core(): lax.ppermute(value, AXES, pairs_of([(0, 1), (1, 0), (2, 3), (3, 2)], 0))  4.6 us
    ppermute x1, starting transfers between devices, local(): crossed = lax.ppermute(merged, AXES, CROSS_PAIRS)  3.1 us
    ppermute x3, waiting for transfers between devices, swap_core(): lax.ppermute(value, AXES, pairs_of([(0, 1), (1, 0), (2, 3), (3, 2)], 0))  2.97 us
    ppermute x1, waiting for transfers between devices, local(): one = lax.ppermute(large, AXES, ONE_PAIRS)  1.65 us
    ppermute x1, starting transfers between devices, local(): lax.ppermute(far[LARGE_ROWS:] + far_in[LARGE_ROWS:], AXES, SMALL_PAIRS)  1.41 us
  transfers between devices with their start and end apart: 7, of which 4 were waited for; matrix products, arithmetic and copies ran while one was open for 0% of the time, Pallas kernels for 3%

profile of v2, /device:TPU:1, one launch (start us, length us, event | category | flops | bytes accessed | tf_op | source)
XLA Modules:
  0.0 39.9 jit_solution(18295923238407125188)
XLA Ops:
  0.0 5.9 %far.1 = (bf16[2048,1024]{1,0:T(8,128)(2,1)S(1)}, bf16[1024,2048]{1,0:T(8,128)(2,1)S(1)}, f32[1296,128]{1,0:T(8,128)S(1)}, f32[1296,128]{1,0:T(8,128)S(1)}) custom-call(s32[6,16]{1,0:T(8,128)} %bitcast.2, bf16[16,128]{1,0:T(8,128)(2,1)} %bitcast.3, bf16[2048,768]{1,0:T(8,128)(2,1)} %jac_ref.1), custom_call_target="tpu_custom_call" | custom-call | flops 1610612736 | bytes 3145728 | tf_op jit(solution)/shard_map/far/pallas_call | solution.py:217
  5.9 3.3 %collective-permute-start.1 = (f32[1296,128]{1,0:T(8,128)S(1)}, f32[1296,128]{1,0:T(8,128)S(1)}, u32[]{:S(2)}, u32[]{:S(2)}) collective-permute-start(f32[1296,128]{1,0:T(8,128)S(1)} %get-tuple-element.16), channel_id=1, source_target_pairs={{0,32},{1,33},{2,34},{3,35},{4,36},{5,37},{6,38},{7,39},{8,40},{9,... | collective-permute-start | bytes 1990664 | tf_op jit(solution)/shard_map/ppermute | solution.py:207
  9.2 1.3 %near.1 = (f32[904,128]{1,0:T(8,128)S(1)}, f32[904,128]{1,0:T(8,128)S(1)}) custom-call(bf16[2048,1024]{1,0:T(8,128)(2,1)S(1)} %get-tuple-element.11.h_ref, bf16[1024,2048]{1,0:T(8,128)(2,1)S(1)} %get-tuple-element.12.at_ref), custom_call_target="tpu_custom_call" | custom-call | flops 1073741824 | tf_op jit(solution)/shard_map/near/pallas_call | solution.py:234
  10.5 0.1 collective-permute-start
  10.6 1.8 %collective-permute-done = f32[904,128]{1,0:T(8,128)S(1)} collective-permute-done((f32[904,128]{1,0:T(8,128)S(1)}, f32[904,128]{1,0:T(8,128)S(1)}, u32[]{:S(2)}, u32[]{:S(2)}) %collective-permute-start) | collective-permute-done | bytes 462880 | tf_op jit(solution)/shard_map/ppermute | solution.py:207
  12.4 0.1 add.32
  12.5 3.1 %collective-permute-start.3 = (f32[904,128]{1,0:T(8,128)S(1)}, f32[904,128]{1,0:T(8,128)S(1)}, u32[]{:S(2)}, u32[]{:S(2)}) collective-permute-start(f32[904,128]{1,0:T(8,128)S(1)} %add.32), channel_id=1, source_target_pairs={{64,32},{65,33},{66,34},{67,35},{68,36},{69,37},{70,38},{71,39},{7... | collective-permute-start | bytes 1388552 | tf_op jit(solution)/shard_map/ppermute | solution.py:245
  15.6 0.0 collective-permute-done.1
  15.6 0.1 slice_add_fusion
  15.6 1.3 %collective-permute-start.2 = (f32[904,128]{1,0:T(8,128)S(1)}, f32[904,128]{1,0:T(8,128)S(1)}, u32[]{:S(2)}, u32[]{:S(2)}) collective-permute-start(f32[904,128]{1,0:T(8,128)S(1)} %slice_add_fusion), channel_id=1, source_target_pairs={{0,1},{1,2},{2,3},{3,4},{4,5},{5,6},{6,7},{7,8},{8,9},{9,10},{10,1... | collective-permute-start | bytes 1388552 | tf_op jit(solution)/shard_map/ppermute | solution.py:247
  17.0 4.7 %collective-permute-start.4 = (f32[776,128]{1,0:T(8,128)S(1)}, f32[776,128]{1,0:T(8,128)S(1)}, u32[]{:S(2)}, u32[]{:S(2)}) collective-permute-start(f32[776,128]{1,0:T(8,128)S(1)} %slice.29), channel_id=1, source_target_pairs={{32,34},{33,35},{34,36},{35,37},{36,38},{37,39},{38,40},{39,41},{4... | collective-permute-start | bytes 1191944 | tf_op jit(solution)/shard_map/ppermute | solution.py:248
  21.7 1.4 %collective-permute-start.5 = (f32[392,128]{1,0:T(8,128)S(1)}, f32[392,128]{1,0:T(8,128)S(1)}, u32[]{:S(2)}, u32[]{:S(2)}) collective-permute-start(f32[392,128]{1,0:T(8,128)S(1)} %slice_add_fusion.1), channel_id=1, source_target_pairs={{0,3},{1,4},{2,5},{3,6},{4,7},{5,8},{6,9},{7,10},{8,11},{9,12},{10... | collective-permute-start | bytes 602120 | tf_op jit(solution)/shard_map/ppermute | solution.py:249
  23.1 11.8 %collective-permute-done.5 = f32[392,128]{1,0:T(8,128)S(1)} collective-permute-done((f32[392,128]{1,0:T(8,128)S(1)}, f32[392,128]{1,0:T(8,128)S(1)}, u32[]{:S(2)}, u32[]{:S(2)}) %collective-permute-start.5) | collective-permute-done | bytes 200736 | tf_op jit(solution)/shard_map/ppermute | solution.py:249
  34.9 0.0 collective-permute-done.3
  34.9 0.0 collective-permute-done.4
  34.9 1.6 %collective-permute-done.2 = f32[904,128]{1,0:T(8,128)S(1)} collective-permute-done((f32[904,128]{1,0:T(8,128)S(1)}, f32[904,128]{1,0:T(8,128)S(1)}, u32[]{:S(2)}, u32[]{:S(2)}) %collective-permute-start.2) | collective-permute-done | bytes 462880 | tf_op jit(solution)/shard_map/ppermute | solution.py:247
  36.5 0.1 pad_add_fusion
  36.7 1.2 %collective-permute-start.6 = (f32[520,128]{1,0:T(8,128)S(1)}, f32[520,128]{1,0:T(8,128)S(1)}, u32[]{:S(2)}, u32[]{:S(2)}) collective-permute-start(f32[520,128]{1,0:T(8,128)S(1)} %get-tuple-element.17), channel_id=1, source_target_pairs={{0,32},{1,33},{2,34},{3,35},{4,36},{5,37},{6,38},{7,39},{8,40},{9,... | collective-permute-start | bytes 798728 | tf_op jit(solution)/shard_map/ppermute | solution.py:207
  37.9 1.2 %collective-permute-done.6.b_ref = f32[520,128]{1,0:T(8,128)S(1)} collective-permute-done((f32[520,128]{1,0:T(8,128)S(1)}, f32[520,128]{1,0:T(8,128)S(1)}, u32[]{:S(2)}, u32[]{:S(2)}) %collective-permute-start.6) | collective-permute-done | bytes 266272 | tf_op jit(solution)/shard_map/ppermute | solution.py:207
  39.0 0.9 %last.1 = f32[256,256]{1,0:T(8,128)} custom-call(f32[520,128]{1,0:T(8,128)S(1)} %get-tuple-element.18.a_ref, f32[520,128]{1,0:T(8,128)S(1)} %collective-permute-done.6.b_ref), custom_call_target="tpu_custom_call" | custom-call | tf_op jit(solution)/shard_map/last/pallas_call | solution.py:257
  (4 shorter events, 0.1 us)
Async XLA Ops:
  5.9 9.7 %collective-permute-start.1 = (f32[1296,128]{1,0:T(8,128)S(1)}, f32[1296,128]{1,0:T(8,128)S(1)}, u32[]{:S(2)}, u32[]{:S(2)}) collective-permute-start(f32[1296,128]{1,0:T(8,128)S(1)} %get-tuple-element.16), channel_id=1, source_target_pairs={{0,32},{1,33},{2,34},{3,35},{4,36},{5,37},{6,38},{7,39},{8,40},{9,... | collective-permute-start | bytes 1990664 | tf_op jit(solution)/shard_map/ppermute | solution.py:207
  10.5 1.9 %collective-permute-start = (f32[904,128]{1,0:T(8,128)S(1)}, f32[904,128]{1,0:T(8,128)S(1)}, u32[]{:S(2)}, u32[]{:S(2)}) collective-permute-start(f32[904,128]{1,0:T(8,128)S(1)} %get-tuple-element.14), channel_id=1, source_target_pairs={{0,32},{1,33},{2,34},{3,35},{4,36},{5,37},{6,38},{7,39},{8,40},{9,... | collective-permute-start | bytes 1388552 | tf_op jit(solution)/shard_map/ppermute | solution.py:207
  12.5 22.4 %collective-permute-start.3 = (f32[904,128]{1,0:T(8,128)S(1)}, f32[904,128]{1,0:T(8,128)S(1)}, u32[]{:S(2)}, u32[]{:S(2)}) collective-permute-start(f32[904,128]{1,0:T(8,128)S(1)} %add.32), channel_id=1, source_target_pairs={{64,32},{65,33},{66,34},{67,35},{68,36},{69,37},{70,38},{71,39},{7... | collective-permute-start | bytes 1388552 | tf_op jit(solution)/shard_map/ppermute | solution.py:245
  15.6 20.9 %collective-permute-start.2 = (f32[904,128]{1,0:T(8,128)S(1)}, f32[904,128]{1,0:T(8,128)S(1)}, u32[]{:S(2)}, u32[]{:S(2)}) collective-permute-start(f32[904,128]{1,0:T(8,128)S(1)} %slice_add_fusion), channel_id=1, source_target_pairs={{0,1},{1,2},{2,3},{3,4},{4,5},{5,6},{6,7},{7,8},{8,9},{9,10},{10,1... | collective-permute-start | bytes 1388552 | tf_op jit(solution)/shard_map/ppermute | solution.py:247
  17.0 17.9 %collective-permute-start.4 = (f32[776,128]{1,0:T(8,128)S(1)}, f32[776,128]{1,0:T(8,128)S(1)}, u32[]{:S(2)}, u32[]{:S(2)}) collective-permute-start(f32[776,128]{1,0:T(8,128)S(1)} %slice.29), channel_id=1, source_target_pairs={{32,34},{33,35},{34,36},{35,37},{36,38},{37,39},{38,40},{39,41},{4... | collective-permute-start | bytes 1191944 | tf_op jit(solution)/shard_map/ppermute | solution.py:248
  21.7 13.2 %collective-permute-start.5 = (f32[392,128]{1,0:T(8,128)S(1)}, f32[392,128]{1,0:T(8,128)S(1)}, u32[]{:S(2)}, u32[]{:S(2)}) collective-permute-start(f32[392,128]{1,0:T(8,128)S(1)} %slice_add_fusion.1), channel_id=1, source_target_pairs={{0,3},{1,4},{2,5},{3,6},{4,7},{5,8},{6,9},{7,10},{8,11},{9,12},{10... | collective-permute-start | bytes 602120 | tf_op jit(solution)/shard_map/ppermute | solution.py:249
  36.7 2.3 %collective-permute-start.6 = (f32[520,128]{1,0:T(8,128)S(1)}, f32[520,128]{1,0:T(8,128)S(1)}, u32[]{:S(2)}, u32[]{:S(2)}) collective-permute-start(f32[520,128]{1,0:T(8,128)S(1)} %get-tuple-element.17), channel_id=1, source_target_pairs={{0,32},{1,33},{2,34},{3,35},{4,36},{5,37},{6,38},{7,39},{8,40},{9,... | collective-permute-start | bytes 798728 | tf_op jit(solution)/shard_map/ppermute | solution.py:207

commit v3 on v2

--- a/solution.py
+++ b/solution.py
@@ -26,8 +26,8 @@
 
 
 SMALL_PAIRS = pairs_of([(0, 0), (3, 1)], 3) + pairs_of([(1, 2), (2, 3)], 1)
-ONE_PAIRS = pairs_of([(0, 0), (3, 1)], 1)
-TWO_PAIRS = pairs_of([(1, 1), (2, 0)], 2)
+ONE_PAIRS = pairs_of([(0, 1), (3, 0)], 1)
+TWO_PAIRS = pairs_of([(1, 0), (2, 1)], 2)
 CROSS_PAIRS = pairs_of([(2, 1), (1, 2)], 0)
 
 
@@ -112,6 +112,8 @@
         rows = slice(part * depth, (part + 1) * depth)
         copies.append(pltpu.make_async_copy(jac_ref.at[rows, :], stage.at[rows, :], sems.at[part]))
         copies[part].start()
+    h_ref[...] = jnp.zeros(h_ref.shape, jnp.bfloat16)
+    at_ref[...] = jnp.zeros(at_ref.shape, jnp.bfloat16)
     cols_copy.wait()
     w_copy.wait()
     weights = w_vmem[...].astype(jnp.float32)
@@ -120,24 +122,13 @@
         if block * BLOCK % depth == 0:
             copies[block * BLOCK // depth].wait()
         rows = slice(block * BLOCK, (block + 1) * BLOCK)
-        total, squares = jnp.int32(0), jnp.int32(0)
         for slot in range(SLOTS):
             offset = jnp.bitwise_and(cols_ref[slot, block] - 2 * home, WINDOW - 1)
-            total, squares = total + offset, squares + offset * offset
             there = pl.ds(pl.multiple_of(offset * BLOCK, BLOCK), BLOCK)
             tile = stage[rows, slot * BLOCK : (slot + 1) * BLOCK]
             h_ref[rows, there] = tile
             turned = tile.T.astype(jnp.float32) * weights[block : block + 1, :]
             at_ref[there, rows] = turned.astype(jnp.bfloat16)
-        total, squares = 28 - total, 140 - squares
-        gap_square = 2 * squares - total * total
-        gap = jnp.int32(0)
-        for step in range(1, SPAN):
-            gap = gap + jnp.where(gap_square >= step * step, 1, 0)
-        for offset in ((total + gap) >> 1, (total - gap) >> 1):
-            there = pl.ds(pl.multiple_of(offset * BLOCK, BLOCK), BLOCK)
-            h_ref[rows, there] = jnp.zeros((BLOCK, BLOCK), jnp.bfloat16)
-            at_ref[there, rows] = jnp.zeros((BLOCK, BLOCK), jnp.bfloat16)
 
     products = {
         distance: jnp.dot(
@@ -154,6 +145,10 @@
 def near_kernel(h_ref, at_ref, keep_ref, send_ref):
     product = jnp.dot(at_ref[...], h_ref[:, 0:256], preferred_element_type=jnp.float32)
     store_group({0: product}, NEAR, 0, 7, lax.axis_index("row") % 2 == 0, keep_ref, send_ref)
+
+
+def merge_kernel(a_ref, b_ref, large_ref, tiny_ref, out_ref):
+    out_ref[...] = a_ref[...] + b_ref[...]
 
 
 def final_kernel(a_ref, b_ref, out_ref, sum_ref):
@@ -241,12 +236,21 @@
         name="near",
     )(h, at)
     near_in = swap_core(near_out)
-    merged = near + near_in
-    crossed = lax.ppermute(merged, AXES, CROSS_PAIRS)
     large = far[:LARGE_ROWS] + far_in[:LARGE_ROWS]
+    tiny = far[LARGE_ROWS:] + far_in[LARGE_ROWS:]
     one = lax.ppermute(large, AXES, ONE_PAIRS)
     two = lax.ppermute(large[:TWO_ROWS], AXES, TWO_PAIRS)
-    small = lax.ppermute(far[LARGE_ROWS:] + far_in[LARGE_ROWS:], AXES, SMALL_PAIRS)
+    small = lax.ppermute(tiny, AXES, SMALL_PAIRS)
+    merged = pl.pallas_call(
+        merge_kernel,
+        out_shape=f32(LARGE_ROWS, BLOCK),
+        in_specs=[VMEM] * 2 + [pl.BlockSpec(memory_space=pl.ANY)] * 2,
+        out_specs=VMEM,
+        compiler_params=PARAMS,
+        cost_estimate=pl.CostEstimate(flops=LARGE_ROWS * BLOCK, bytes_accessed=0, transcendentals=0),
+        name="merge",
+    )(near, near_in, large, tiny)
+    crossed = lax.ppermute(merged, AXES, CROSS_PAIRS)
     total = jnp.where(owns, merged, 0.0) + one + crossed
     total = total + jnp.pad(two, ((0, LARGE_ROWS - TWO_ROWS), (0, 0)))
     total = total + jnp.pad(small, ((0, LARGE_ROWS - SMALL_ROWS), (0, 0)))

time: 40.3 us -> 38.8 us (0.963)
  waiting for transfers between devices: 16.4 us -> 13.5 us
  starting transfers between devices: 15.1 us -> 17.2 us
  Pallas kernels: 8.02 us -> 7.43 us
    ppermute x1, starting transfers between devices: 4.66 us -> 6.46 us  [local(): two = lax.ppermute(large[:TWO_ROWS], AXES, TWO_PAIRS)]
    ppermute x1, waiting for transfers between devices: 1.65 us -> 0.01 us  [local(): one = lax.ppermute(large, AXES, ONE_PAIRS)]
    ppermute x1, waiting for transfers between devices: 11.8 us -> 10.6 us  [local(): small = lax.ppermute(tiny, AXES, SMALL_PAIRS)]
    pallas_call x1, Pallas kernels: 5.87 us -> 5.23 us  [local(): pl.pallas_call(far_kernel, out_shape=(bf16(rows, 1024), bf16(1024, rows),...]
where the time goes in v3:
time: 38.8 us; the launch traced here: 38.4 us
  starting transfers between devices  17.2 us (44%)
  waiting for transfers between devices  13.5 us (35%)
  Pallas kernels  7.43 us (19%)
    ppermute x1, waiting for transfers between devices, local(): small = lax.ppermute(tiny, AXES, SMALL_PAIRS)  10.6 us
    ppermute x1, starting transfers between devices, local(): two = lax.ppermute(large[:TWO_ROWS], AXES, TWO_PAIRS)  6.46 us
    pallas_call x1, Pallas kernels, local(): pl.pallas_call(far_kernel, out_shape=(bf16(rows, 1024), bf16(1024, rows),...  5.23 us
    ppermute x3, starting transfers between devices, swap_core(): lax.ppermute(value, AXES, pairs_of([(0, 1), (1, 0), (2, 3), (3, 2)], 0))  4.98 us
    ppermute x1, starting transfers between devices, local(): crossed = lax.ppermute(merged, AXES, CROSS_PAIRS)  3.13 us
    ppermute x3, waiting for transfers between devices, swap_core(): lax.ppermute(value, AXES, pairs_of([(0, 1), (1, 0), (2, 3), (3, 2)], 0))  2.87 us
    ppermute x1, starting transfers between devices, local(): one = lax.ppermute(large, AXES, ONE_PAIRS)  1.29 us
    ppermute x1, starting transfers between devices, local(): small = lax.ppermute(tiny, AXES, SMALL_PAIRS)  1.29 us
  transfers between devices with their start and end apart: 7, of which 4 were waited for; matrix products, arithmetic and copies ran while one was open for 0% of the time, Pallas kernels for 3%

profile of v3, /device:TPU:1, one launch (start us, length us, event | category | flops | bytes accessed | tf_op | source)
XLA Modules:
  0.0 38.4 jit_solution(9888635188673046422)
XLA Ops:
  0.0 5.2 %far.1 = (bf16[2048,1024]{1,0:T(8,128)(2,1)S(1)}, bf16[1024,2048]{1,0:T(8,128)(2,1)S(1)}, f32[1296,128]{1,0:T(8,128)S(1)}, f32[1296,128]{1,0:T(8,128)S(1)}) custom-call(s32[6,16]{1,0:T(8,128)} %bitcast.2, bf16[16,128]{1,0:T(8,128)(2,1)} %bitcast.3, bf16[2048,768]{1,0:T(8,128)(2,1)} %jac_ref.1), custom_call_target="tpu_custom_call" | custom-call | flops 1610612736 | bytes 3145728 | tf_op jit(solution)/shard_map/far/pallas_call | solution.py:212
  5.2 3.3 %collective-permute-start.1 = (f32[1296,128]{1,0:T(8,128)S(1)}, f32[1296,128]{1,0:T(8,128)S(1)}, u32[]{:S(2)}, u32[]{:S(2)}) collective-permute-start(f32[1296,128]{1,0:T(8,128)S(1)} %get-tuple-element.16), channel_id=1, source_target_pairs={{0,32},{1,33},{2,34},{3,35},{4,36},{5,37},{6,38},{7,39},{8,40},{9,... | collective-permute-start | bytes 1990664 | tf_op jit(solution)/shard_map/ppermute | solution.py:202
  8.5 1.3 %near.1 = (f32[904,128]{1,0:T(8,128)S(1)}, f32[904,128]{1,0:T(8,128)S(1)}) custom-call(bf16[2048,1024]{1,0:T(8,128)(2,1)S(1)} %get-tuple-element.11.h_ref, bf16[1024,2048]{1,0:T(8,128)(2,1)S(1)} %get-tuple-element.12.at_ref), custom_call_target="tpu_custom_call" | custom-call | flops 1073741824 | tf_op jit(solution)/shard_map/near/pallas_call | solution.py:229
  9.8 0.1 collective-permute-start
  9.9 0.4 collective-permute-done.1
  10.3 0.1 slice_add_fusion.large_ref
  10.4 1.4 %collective-permute-done.b_ref = f32[904,128]{1,0:T(8,128)S(1)} collective-permute-done((f32[904,128]{1,0:T(8,128)S(1)}, f32[904,128]{1,0:T(8,128)S(1)}, u32[]{:S(2)}, u32[]{:S(2)}) %collective-permute-start) | collective-permute-done | bytes 462880 | tf_op jit(solution)/shard_map/ppermute | solution.py:202
  11.8 3.1 %collective-permute-start.3 = (f32[904,128]{1,0:T(8,128)S(1)}, f32[904,128]{1,0:T(8,128)S(1)}, u32[]{:S(2)}, u32[]{:S(2)}) collective-permute-start(f32[904,128]{1,0:T(8,128)S(1)} %merge.1), channel_id=1, source_target_pairs={{64,32},{65,33},{66,34},{67,35},{68,36},{69,37},{70,38},{71,39},{7... | collective-permute-start | bytes 1388552 | tf_op jit(solution)/shard_map/ppermute | solution.py:253
  14.9 1.3 %collective-permute-start.2 = (f32[904,128]{1,0:T(8,128)S(1)}, f32[904,128]{1,0:T(8,128)S(1)}, u32[]{:S(2)}, u32[]{:S(2)}) collective-permute-start(f32[904,128]{1,0:T(8,128)S(1)} %slice_add_fusion.large_ref), channel_id=1, source_target_pairs={{0,33},{1,34},{2,35},{3,36},{4,37},{5,38},{6,39},{7,40},{8,41},{9,... | collective-permute-start | bytes 1388552 | tf_op jit(solution)/shard_map/ppermute | solution.py:241
  16.3 6.5 %collective-permute-start.4 = (f32[776,128]{1,0:T(8,128)S(1)}, f32[776,128]{1,0:T(8,128)S(1)}, u32[]{:S(2)}, u32[]{:S(2)}) collective-permute-start(f32[776,128]{1,0:T(8,128)S(1)} %slice.30), channel_id=1, source_target_pairs={{32,2},{33,3},{34,4},{35,5},{36,6},{37,7},{38,8},{39,9},{40,10},{4... | collective-permute-start | bytes 1191944 | tf_op jit(solution)/shard_map/ppermute | solution.py:242
  22.7 1.3 %collective-permute-start.5 = (f32[392,128]{1,0:T(8,128)S(1)}, f32[392,128]{1,0:T(8,128)S(1)}, u32[]{:S(2)}, u32[]{:S(2)}) collective-permute-start(f32[392,128]{1,0:T(8,128)S(1)} %slice_add_fusion.1.tiny_ref), channel_id=1, source_target_pairs={{0,3},{1,4},{2,5},{3,6},{4,7},{5,8},{6,9},{7,10},{8,11},{9,12},{10... | collective-permute-start | bytes 602120 | tf_op jit(solution)/shard_map/ppermute | solution.py:243
  24.0 10.6 %collective-permute-done.5 = f32[392,128]{1,0:T(8,128)S(1)} collective-permute-done((f32[392,128]{1,0:T(8,128)S(1)}, f32[392,128]{1,0:T(8,128)S(1)}, u32[]{:S(2)}, u32[]{:S(2)}) %collective-permute-start.5) | collective-permute-done | bytes 200736 | tf_op jit(solution)/shard_map/ppermute | solution.py:243
  34.6 0.0 collective-permute-done.4
  34.6 0.0 collective-permute-done.3
  34.6 0.0 collective-permute-done.2
  34.6 0.1 pad_add_fusion
  34.8 1.6 %collective-permute-start.6 = (f32[520,128]{1,0:T(8,128)S(1)}, f32[520,128]{1,0:T(8,128)S(1)}, u32[]{:S(2)}, u32[]{:S(2)}) collective-permute-start(f32[520,128]{1,0:T(8,128)S(1)} %get-tuple-element.17), channel_id=1, source_target_pairs={{0,32},{1,33},{2,34},{3,35},{4,36},{5,37},{6,38},{7,39},{8,40},{9,... | collective-permute-start | bytes 798728 | tf_op jit(solution)/shard_map/ppermute | solution.py:202
  36.4 1.2 %collective-permute-done.6.b_ref = f32[520,128]{1,0:T(8,128)S(1)} collective-permute-done((f32[520,128]{1,0:T(8,128)S(1)}, f32[520,128]{1,0:T(8,128)S(1)}, u32[]{:S(2)}, u32[]{:S(2)}) %collective-permute-start.6) | collective-permute-done | bytes 266272 | tf_op jit(solution)/shard_map/ppermute | solution.py:202
  37.5 0.9 %last.1 = f32[256,256]{1,0:T(8,128)} custom-call(f32[520,128]{1,0:T(8,128)S(1)} %get-tuple-element.18.a_ref, f32[520,128]{1,0:T(8,128)S(1)} %collective-permute-done.6.b_ref), custom_call_target="tpu_custom_call" | custom-call | tf_op jit(solution)/shard_map/last/pallas_call | solution.py:261
  (5 shorter events, 0.2 us)
Async XLA Ops:
  5.2 5.0 %collective-permute-start.1 = (f32[1296,128]{1,0:T(8,128)S(1)}, f32[1296,128]{1,0:T(8,128)S(1)}, u32[]{:S(2)}, u32[]{:S(2)}) collective-permute-start(f32[1296,128]{1,0:T(8,128)S(1)} %get-tuple-element.16), channel_id=1, source_target_pairs={{0,32},{1,33},{2,34},{3,35},{4,36},{5,37},{6,38},{7,39},{8,40},{9,... | collective-permute-start | bytes 1990664 | tf_op jit(solution)/shard_map/ppermute | solution.py:202
  9.8 1.9 %collective-permute-start = (f32[904,128]{1,0:T(8,128)S(1)}, f32[904,128]{1,0:T(8,128)S(1)}, u32[]{:S(2)}, u32[]{:S(2)}) collective-permute-start(f32[904,128]{1,0:T(8,128)S(1)} %get-tuple-element.14), channel_id=1, source_target_pairs={{0,32},{1,33},{2,34},{3,35},{4,36},{5,37},{6,38},{7,39},{8,40},{9,... | collective-permute-start | bytes 1388552 | tf_op jit(solution)/shard_map/ppermute | solution.py:202
  11.8 22.8 %collective-permute-start.3 = (f32[904,128]{1,0:T(8,128)S(1)}, f32[904,128]{1,0:T(8,128)S(1)}, u32[]{:S(2)}, u32[]{:S(2)}) collective-permute-start(f32[904,128]{1,0:T(8,128)S(1)} %merge.1), channel_id=1, source_target_pairs={{64,32},{65,33},{66,34},{67,35},{68,36},{69,37},{70,38},{71,39},{7... | collective-permute-start | bytes 1388552 | tf_op jit(solution)/shard_map/ppermute | solution.py:253
  14.9 19.7 %collective-permute-start.2 = (f32[904,128]{1,0:T(8,128)S(1)}, f32[904,128]{1,0:T(8,128)S(1)}, u32[]{:S(2)}, u32[]{:S(2)}) collective-permute-start(f32[904,128]{1,0:T(8,128)S(1)} %slice_add_fusion.large_ref), channel_id=1, source_target_pairs={{0,33},{1,34},{2,35},{3,36},{4,37},{5,38},{6,39},{7,40},{8,41},{9,... | collective-permute-start | bytes 1388552 | tf_op jit(solution)/shard_map/ppermute | solution.py:241
  16.3 18.3 %collective-permute-start.4 = (f32[776,128]{1,0:T(8,128)S(1)}, f32[776,128]{1,0:T(8,128)S(1)}, u32[]{:S(2)}, u32[]{:S(2)}) collective-permute-start(f32[776,128]{1,0:T(8,128)S(1)} %slice.30), channel_id=1, source_target_pairs={{32,2},{33,3},{34,4},{35,5},{36,6},{37,7},{38,8},{39,9},{40,10},{4... | collective-permute-start | bytes 1191944 | tf_op jit(solution)/shard_map/ppermute | solution.py:242
  22.7 11.9 %collective-permute-start.5 = (f32[392,128]{1,0:T(8,128)S(1)}, f32[392,128]{1,0:T(8,128)S(1)}, u32[]{:S(2)}, u32[]{:S(2)}) collective-permute-start(f32[392,128]{1,0:T(8,128)S(1)} %slice_add_fusion.1.tiny_ref), channel_id=1, source_target_pairs={{0,3},{1,4},{2,5},{3,6},{4,7},{5,8},{6,9},{7,10},{8,11},{9,12},{10... | collective-permute-start | bytes 602120 | tf_op jit(solution)/shard_map/ppermute | solution.py:243
  34.8 2.7 %collective-permute-start.6 = (f32[520,128]{1,0:T(8,128)S(1)}, f32[520,128]{1,0:T(8,128)S(1)}, u32[]{:S(2)}, u32[]{:S(2)}) collective-permute-start(f32[520,128]{1,0:T(8,128)S(1)} %get-tuple-element.17), channel_id=1, source_target_pairs={{0,32},{1,33},{2,34},{3,35},{4,36},{5,37},{6,38},{7,39},{8,40},{9,... | collective-permute-start | bytes 798728 | tf_op jit(solution)/shard_map/ppermute | solution.py:202

commit v4 on v3

--- a/solution.py
+++ b/solution.py
@@ -25,7 +25,7 @@
     ]
 
 
-SMALL_PAIRS = pairs_of([(0, 0), (3, 1)], 3) + pairs_of([(1, 2), (2, 3)], 1)
+SMALL_PAIRS = pairs_of([(0, 0), (3, 1)], 3) + pairs_of([(1, 3), (2, 2)], 1)
 ONE_PAIRS = pairs_of([(0, 1), (3, 0)], 1)
 TWO_PAIRS = pairs_of([(1, 0), (2, 1)], 2)
 CROSS_PAIRS = pairs_of([(2, 1), (1, 2)], 0)
@@ -218,7 +218,7 @@
             pltpu.VMEM(jac_values.shape, jnp.bfloat16),
             pltpu.SMEM((SLOTS, rows // BLOCK), jnp.int32),
             pltpu.VMEM((rows // BLOCK, BLOCK), jnp.bfloat16),
-            pltpu.SemaphoreType.DMA((4,)),
+            pltpu.SemaphoreType.DMA((2,)),
             pltpu.SemaphoreType.DMA((2,)),
         ],
         compiler_params=PARAMS,

time: 38.8 us -> 38.5 us (level)
  starting transfers between devices: 17.2 us -> 15.9 us
  waiting for transfers between devices: 13.5 us -> 14.6 us
    ppermute x1, starting transfers between devices: 1.29 us -> 0.08 us  [local(): small = lax.ppermute(tiny, AXES, SMALL_PAIRS)]
    ppermute x1, waiting for transfers between devices: 10.6 us -> 11.7 us  [local(): small = lax.ppermute(tiny, AXES, SMALL_PAIRS)]
where the time goes in v4:
time: 38.5 us; the launch traced here: 38.3 us
  starting transfers between devices  15.9 us (41%)
  waiting for transfers between devices  14.6 us (38%)
  Pallas kernels  7.31 us (19%)
    ppermute x1, waiting for transfers between devices, local(): small = lax.ppermute(tiny, AXES, SMALL_PAIRS)  11.7 us
    ppermute x1, starting transfers between devices, local(): two = lax.ppermute(large[:TWO_ROWS], AXES, TWO_PAIRS)  6.47 us
    pallas_call x1, Pallas kernels, local(): pl.pallas_call(far_kernel, out_shape=(bf16(rows, 1024), bf16(1024, rows),...  5.11 us
    ppermute x3, starting transfers between devices, swap_core(): lax.ppermute(value, AXES, pairs_of([(0, 1), (1, 0), (2, 3), (3, 2)], 0))  4.97 us
    ppermute x1, starting transfers between devices, local(): crossed = lax.ppermute(merged, AXES, CROSS_PAIRS)  3.11 us
    ppermute x3, waiting for transfers between devices, swap_core(): lax.ppermute(value, AXES, pairs_of([(0, 1), (1, 0), (2, 3), (3, 2)], 0))  2.88 us
    ppermute x1, starting transfers between devices, local(): one = lax.ppermute(large, AXES, ONE_PAIRS)  1.29 us
    pallas_call x1, Pallas kernels, local(): pl.pallas_call(near_kernel, out_shape=(f32(LARGE_ROWS, BLOCK), f32(LARGE_...  1.27 us
  transfers between devices with their start and end apart: 7, of which 4 were waited for; matrix products, arithmetic and copies ran while one was open for 0% of the time, Pallas kernels for 3%

profile of v4, /device:TPU:1, one launch (start us, length us, event | category | flops | bytes accessed | tf_op | source)
XLA Modules:
  0.0 38.3 jit_solution(1200640864997552838)
XLA Ops:
  0.0 5.1 %far.1 = (bf16[2048,1024]{1,0:T(8,128)(2,1)S(1)}, bf16[1024,2048]{1,0:T(8,128)(2,1)S(1)}, f32[1296,128]{1,0:T(8,128)S(1)}, f32[1296,128]{1,0:T(8,128)S(1)}) custom-call(s32[6,16]{1,0:T(8,128)} %bitcast.2, bf16[16,128]{1,0:T(8,128)(2,1)} %bitcast.3, bf16[2048,768]{1,0:T(8,128)(2,1)} %jac_ref.1), custom_call_target="tpu_custom_call" | custom-call | flops 1610612736 | bytes 3145728 | tf_op jit(solution)/shard_map/far/pallas_call | solution.py:212
  5.1 3.3 %collective-permute-start.1 = (f32[1296,128]{1,0:T(8,128)S(1)}, f32[1296,128]{1,0:T(8,128)S(1)}, u32[]{:S(2)}, u32[]{:S(2)}) collective-permute-start(f32[1296,128]{1,0:T(8,128)S(1)} %get-tuple-element.16), channel_id=1, source_target_pairs={{0,32},{1,33},{2,34},{3,35},{4,36},{5,37},{6,38},{7,39},{8,40},{9,... | collective-permute-start | bytes 1990664 | tf_op jit(solution)/shard_map/ppermute | solution.py:202
  8.4 1.3 %near.1 = (f32[904,128]{1,0:T(8,128)S(1)}, f32[904,128]{1,0:T(8,128)S(1)}) custom-call(bf16[2048,1024]{1,0:T(8,128)(2,1)S(1)} %get-tuple-element.11.h_ref, bf16[1024,2048]{1,0:T(8,128)(2,1)S(1)} %get-tuple-element.12.at_ref), custom_call_target="tpu_custom_call" | custom-call | flops 1073741824 | tf_op jit(solution)/shard_map/near/pallas_call | solution.py:229
  9.7 0.1 collective-permute-start
  9.8 0.4 collective-permute-done.1
  10.2 0.1 slice_add_fusion.large_ref
  10.3 1.4 %collective-permute-done.b_ref = f32[904,128]{1,0:T(8,128)S(1)} collective-permute-done((f32[904,128]{1,0:T(8,128)S(1)}, f32[904,128]{1,0:T(8,128)S(1)}, u32[]{:S(2)}, u32[]{:S(2)}) %collective-permute-start) | collective-permute-done | bytes 462880 | tf_op jit(solution)/shard_map/ppermute | solution.py:202
  11.7 3.1 %collective-permute-start.3 = (f32[904,128]{1,0:T(8,128)S(1)}, f32[904,128]{1,0:T(8,128)S(1)}, u32[]{:S(2)}, u32[]{:S(2)}) collective-permute-start(f32[904,128]{1,0:T(8,128)S(1)} %merge.1), channel_id=1, source_target_pairs={{64,32},{65,33},{66,34},{67,35},{68,36},{69,37},{70,38},{71,39},{7... | collective-permute-start | bytes 1388552 | tf_op jit(solution)/shard_map/ppermute | solution.py:253
  14.8 1.3 %collective-permute-start.2 = (f32[904,128]{1,0:T(8,128)S(1)}, f32[904,128]{1,0:T(8,128)S(1)}, u32[]{:S(2)}, u32[]{:S(2)}) collective-permute-start(f32[904,128]{1,0:T(8,128)S(1)} %slice_add_fusion.large_ref), channel_id=1, source_target_pairs={{0,33},{1,34},{2,35},{3,36},{4,37},{5,38},{6,39},{7,40},{8,41},{9,... | collective-permute-start | bytes 1388552 | tf_op jit(solution)/shard_map/ppermute | solution.py:241
  16.1 6.5 %collective-permute-start.4 = (f32[776,128]{1,0:T(8,128)S(1)}, f32[776,128]{1,0:T(8,128)S(1)}, u32[]{:S(2)}, u32[]{:S(2)}) collective-permute-start(f32[776,128]{1,0:T(8,128)S(1)} %slice.30), channel_id=1, source_target_pairs={{32,2},{33,3},{34,4},{35,5},{36,6},{37,7},{38,8},{39,9},{40,10},{4... | collective-permute-start | bytes 1191944 | tf_op jit(solution)/shard_map/ppermute | solution.py:242
  22.6 0.1 collective-permute-start.5
  22.7 11.7 %collective-permute-done.5 = f32[392,128]{1,0:T(8,128)S(1)} collective-permute-done((f32[392,128]{1,0:T(8,128)S(1)}, f32[392,128]{1,0:T(8,128)S(1)}, u32[]{:S(2)}, u32[]{:S(2)}) %collective-permute-start.5) | collective-permute-done | bytes 200736 | tf_op jit(solution)/shard_map/ppermute | solution.py:243
  34.5 0.0 collective-permute-done.4
  34.5 0.0 collective-permute-done.3
  34.5 0.0 collective-permute-done.2
  34.5 0.1 pad_add_fusion
  34.7 1.6 %collective-permute-start.6 = (f32[520,128]{1,0:T(8,128)S(1)}, f32[520,128]{1,0:T(8,128)S(1)}, u32[]{:S(2)}, u32[]{:S(2)}) collective-permute-start(f32[520,128]{1,0:T(8,128)S(1)} %get-tuple-element.17), channel_id=1, source_target_pairs={{0,32},{1,33},{2,34},{3,35},{4,36},{5,37},{6,38},{7,39},{8,40},{9,... | collective-permute-start | bytes 798728 | tf_op jit(solution)/shard_map/ppermute | solution.py:202
  36.2 1.2 %collective-permute-done.6.b_ref = f32[520,128]{1,0:T(8,128)S(1)} collective-permute-done((f32[520,128]{1,0:T(8,128)S(1)}, f32[520,128]{1,0:T(8,128)S(1)}, u32[]{:S(2)}, u32[]{:S(2)}) %collective-permute-start.6) | collective-permute-done | bytes 266272 | tf_op jit(solution)/shard_map/ppermute | solution.py:202
  37.4 0.9 %last.1 = f32[256,256]{1,0:T(8,128)} custom-call(f32[520,128]{1,0:T(8,128)S(1)} %get-tuple-element.18.a_ref, f32[520,128]{1,0:T(8,128)S(1)} %collective-permute-done.6.b_ref), custom_call_target="tpu_custom_call" | custom-call | tf_op jit(solution)/shard_map/last/pallas_call | solution.py:261
  (5 shorter events, 0.2 us)
Async XLA Ops:
  5.1 5.0 %collective-permute-start.1 = (f32[1296,128]{1,0:T(8,128)S(1)}, f32[1296,128]{1,0:T(8,128)S(1)}, u32[]{:S(2)}, u32[]{:S(2)}) collective-permute-start(f32[1296,128]{1,0:T(8,128)S(1)} %get-tuple-element.16), channel_id=1, source_target_pairs={{0,32},{1,33},{2,34},{3,35},{4,36},{5,37},{6,38},{7,39},{8,40},{9,... | collective-permute-start | bytes 1990664 | tf_op jit(solution)/shard_map/ppermute | solution.py:202
  9.7 1.9 %collective-permute-start = (f32[904,128]{1,0:T(8,128)S(1)}, f32[904,128]{1,0:T(8,128)S(1)}, u32[]{:S(2)}, u32[]{:S(2)}) collective-permute-start(f32[904,128]{1,0:T(8,128)S(1)} %get-tuple-element.14), channel_id=1, source_target_pairs={{0,32},{1,33},{2,34},{3,35},{4,36},{5,37},{6,38},{7,39},{8,40},{9,... | collective-permute-start | bytes 1388552 | tf_op jit(solution)/shard_map/ppermute | solution.py:202
  11.7 22.8 %collective-permute-start.3 = (f32[904,128]{1,0:T(8,128)S(1)}, f32[904,128]{1,0:T(8,128)S(1)}, u32[]{:S(2)}, u32[]{:S(2)}) collective-permute-start(f32[904,128]{1,0:T(8,128)S(1)} %merge.1), channel_id=1, source_target_pairs={{64,32},{65,33},{66,34},{67,35},{68,36},{69,37},{70,38},{71,39},{7... | collective-permute-start | bytes 1388552 | tf_op jit(solution)/shard_map/ppermute | solution.py:253
  14.8 19.7 %collective-permute-start.2 = (f32[904,128]{1,0:T(8,128)S(1)}, f32[904,128]{1,0:T(8,128)S(1)}, u32[]{:S(2)}, u32[]{:S(2)}) collective-permute-start(f32[904,128]{1,0:T(8,128)S(1)} %slice_add_fusion.large_ref), channel_id=1, source_target_pairs={{0,33},{1,34},{2,35},{3,36},{4,37},{5,38},{6,39},{7,40},{8,41},{9,... | collective-permute-start | bytes 1388552 | tf_op jit(solution)/shard_map/ppermute | solution.py:241
  16.1 18.3 %collective-permute-start.4 = (f32[776,128]{1,0:T(8,128)S(1)}, f32[776,128]{1,0:T(8,128)S(1)}, u32[]{:S(2)}, u32[]{:S(2)}) collective-permute-start(f32[776,128]{1,0:T(8,128)S(1)} %slice.30), channel_id=1, source_target_pairs={{32,2},{33,3},{34,4},{35,5},{36,6},{37,7},{38,8},{39,9},{40,10},{4... | collective-permute-start | bytes 1191944 | tf_op jit(solution)/shard_map/ppermute | solution.py:242
  22.6 11.9 %collective-permute-start.5 = (f32[392,128]{1,0:T(8,128)S(1)}, f32[392,128]{1,0:T(8,128)S(1)}, u32[]{:S(2)}, u32[]{:S(2)}) collective-permute-start(f32[392,128]{1,0:T(8,128)S(1)} %slice_add_fusion.1.tiny_ref), channel_id=1, source_target_pairs={{0,3},{1,4},{2,5},{3,6},{4,7},{5,8},{6,9},{7,10},{8,11},{9,12},{10... | collective-permute-start | bytes 602120 | tf_op jit(solution)/shard_map/ppermute | solution.py:243
  34.7 2.7 %collective-permute-start.6 = (f32[520,128]{1,0:T(8,128)S(1)}, f32[520,128]{1,0:T(8,128)S(1)}, u32[]{:S(2)}, u32[]{:S(2)}) collective-permute-start(f32[520,128]{1,0:T(8,128)S(1)} %get-tuple-element.17), channel_id=1, source_target_pairs={{0,32},{1,33},{2,34},{3,35},{4,36},{5,37},{6,38},{7,39},{8,40},{9,... | collective-permute-start | bytes 798728 | tf_op jit(solution)/shard_map/ppermute | solution.py:202

commit v5 on v4

--- a/solution.py
+++ b/solution.py
@@ -147,7 +147,7 @@
     store_group({0: product}, NEAR, 0, 7, lax.axis_index("row") % 2 == 0, keep_ref, send_ref)
 
 
-def merge_kernel(a_ref, b_ref, large_ref, tiny_ref, out_ref):
+def merge_kernel(a_ref, b_ref, out_ref):
     out_ref[...] = a_ref[...] + b_ref[...]
 
 
@@ -236,21 +236,20 @@
         name="near",
     )(h, at)
     near_in = swap_core(near_out)
-    large = far[:LARGE_ROWS] + far_in[:LARGE_ROWS]
-    tiny = far[LARGE_ROWS:] + far_in[LARGE_ROWS:]
-    one = lax.ppermute(large, AXES, ONE_PAIRS)
-    two = lax.ppermute(large[:TWO_ROWS], AXES, TWO_PAIRS)
-    small = lax.ppermute(tiny, AXES, SMALL_PAIRS)
     merged = pl.pallas_call(
         merge_kernel,
         out_shape=f32(LARGE_ROWS, BLOCK),
-        in_specs=[VMEM] * 2 + [pl.BlockSpec(memory_space=pl.ANY)] * 2,
+        in_specs=[VMEM] * 2,
         out_specs=VMEM,
         compiler_params=PARAMS,
-        cost_estimate=pl.CostEstimate(flops=LARGE_ROWS * BLOCK, bytes_accessed=0, transcendentals=0),
+        cost_estimate=pl.CostEstimate(flops=20000000000, bytes_accessed=0, transcendentals=0),
         name="merge",
-    )(near, near_in, large, tiny)
+    )(near, near_in)
     crossed = lax.ppermute(merged, AXES, CROSS_PAIRS)
+    large = far[:LARGE_ROWS] + far_in[:LARGE_ROWS]
+    one = lax.ppermute(large, AXES, ONE_PAIRS)
+    two = lax.ppermute(large[:TWO_ROWS], AXES, TWO_PAIRS)
+    small = lax.ppermute(far[LARGE_ROWS:] + far_in[LARGE_ROWS:], AXES, SMALL_PAIRS)
     total = jnp.where(owns, merged, 0.0) + one + crossed
     total = total + jnp.pad(two, ((0, LARGE_ROWS - TWO_ROWS), (0, 0)))
     total = total + jnp.pad(small, ((0, LARGE_ROWS - SMALL_ROWS), (0, 0)))

time: 38.5 us -> 38.3 us (level)
  waiting for transfers between devices: 14.6 us -> 14.2 us
  transfers between devices with their start and end apart: 7 -> 7, of which waited for: 4 -> 3; matrix products, arithmetic and copies ran while one was open for 0% -> 0% of each run, Pallas kernels for 3% -> 0%
where the time goes in v5:
time: 38.3 us; the launch traced here: 38.2 us
  starting transfers between devices  16.2 us (42%)
  waiting for transfers between devices  14.2 us (37%)
  Pallas kernels  7.31 us (19%)
    ppermute x1, waiting for transfers between devices, local(): lax.ppermute(far[LARGE_ROWS:] + far_in[LARGE_ROWS:], AXES, SMALL_PAIRS)  11.7 us
    ppermute x1, starting transfers between devices, local(): two = lax.ppermute(large[:TWO_ROWS], AXES, TWO_PAIRS)  6.47 us
    pallas_call x1, Pallas kernels, local(): pl.pallas_call(far_kernel, out_shape=(bf16(rows, 1024), bf16(1024, rows),...  5.11 us
    ppermute x3, starting transfers between devices, swap_core(): lax.ppermute(value, AXES, pairs_of([(0, 1), (1, 0), (2, 3), (3, 2)], 0))  5.06 us
    ppermute x1, starting transfers between devices, local(): crossed = lax.ppermute(merged, AXES, CROSS_PAIRS)  3.33 us
    ppermute x3, waiting for transfers between devices, swap_core(): lax.ppermute(value, AXES, pairs_of([(0, 1), (1, 0), (2, 3), (3, 2)], 0))  2.52 us
    ppermute x1, starting transfers between devices, local(): one = lax.ppermute(large, AXES, ONE_PAIRS)  1.29 us
    pallas_call x1, Pallas kernels, local(): pl.pallas_call(near_kernel, out_shape=(f32(LARGE_ROWS, BLOCK), f32(LARGE_...  1.27 us
  transfers between devices with their start and end apart: 7, of which 3 were waited for; matrix products, arithmetic and copies ran while one was open for 0% of the time, Pallas kernels for 0%

profile of v5, /device:TPU:1, one launch (start us, length us, event | category | flops | bytes accessed | tf_op | source)
XLA Modules:
  0.0 38.2 jit_solution(2368690516083336492)
XLA Ops:
  0.0 5.1 %far.1 = (bf16[2048,1024]{1,0:T(8,128)(2,1)S(1)}, bf16[1024,2048]{1,0:T(8,128)(2,1)S(1)}, f32[1296,128]{1,0:T(8,128)S(1)}, f32[1296,128]{1,0:T(8,128)S(1)}) custom-call(s32[6,16]{1,0:T(8,128)} %bitcast.2, bf16[16,128]{1,0:T(8,128)(2,1)} %bitcast.3, bf16[2048,768]{1,0:T(8,128)(2,1)} %jac_ref.1), custom_call_target="tpu_custom_call" | custom-call | flops 1610612736 | bytes 3145728 | tf_op jit(solution)/shard_map/far/pallas_call | solution.py:212
  5.1 1.3 %near.1 = (f32[904,128]{1,0:T(8,128)S(1)}, f32[904,128]{1,0:T(8,128)S(1)}) custom-call(bf16[2048,1024]{1,0:T(8,128)(2,1)S(1)} %get-tuple-element.11.h_ref, bf16[1024,2048]{1,0:T(8,128)(2,1)S(1)} %get-tuple-element.12.at_ref), custom_call_target="tpu_custom_call" | custom-call | flops 1073741824 | tf_op jit(solution)/shard_map/near/pallas_call | solution.py:229
  6.4 3.3 %collective-permute-start = (f32[904,128]{1,0:T(8,128)S(1)}, f32[904,128]{1,0:T(8,128)S(1)}, u32[]{:S(2)}, u32[]{:S(2)}) collective-permute-start(f32[904,128]{1,0:T(8,128)S(1)} %get-tuple-element.14), channel_id=1, source_target_pairs={{0,32},{1,33},{2,34},{3,35},{4,36},{5,37},{6,38},{7,39},{8,40},{9,... | collective-permute-start | bytes 1388552 | tf_op jit(solution)/shard_map/ppermute | solution.py:202
  9.7 0.1 collective-permute-start.1
  9.8 1.3 %collective-permute-done.b_ref = f32[904,128]{1,0:T(8,128)S(1)} collective-permute-done((f32[904,128]{1,0:T(8,128)S(1)}, f32[904,128]{1,0:T(8,128)S(1)}, u32[]{:S(2)}, u32[]{:S(2)}) %collective-permute-start) | collective-permute-done | bytes 462880 | tf_op jit(solution)/shard_map/ppermute | solution.py:202
  11.2 3.3 %collective-permute-start.3 = (f32[904,128]{1,0:T(8,128)S(1)}, f32[904,128]{1,0:T(8,128)S(1)}, u32[]{:S(2)}, u32[]{:S(2)}) collective-permute-start(f32[904,128]{1,0:T(8,128)S(1)} %merge.1), channel_id=1, source_target_pairs={{64,32},{65,33},{66,34},{67,35},{68,36},{69,37},{70,38},{71,39},{7... | collective-permute-start | bytes 1388552 | tf_op jit(solution)/shard_map/ppermute | solution.py:248
  14.6 0.0 collective-permute-done.1
  14.6 0.1 slice_add_fusion
  14.7 1.3 %collective-permute-start.2 = (f32[904,128]{1,0:T(8,128)S(1)}, f32[904,128]{1,0:T(8,128)S(1)}, u32[]{:S(2)}, u32[]{:S(2)}) collective-permute-start(f32[904,128]{1,0:T(8,128)S(1)} %slice_add_fusion), channel_id=1, source_target_pairs={{0,33},{1,34},{2,35},{3,36},{4,37},{5,38},{6,39},{7,40},{8,41},{9,... | collective-permute-start | bytes 1388552 | tf_op jit(solution)/shard_map/ppermute | solution.py:250
  16.0 6.5 %collective-permute-start.4 = (f32[776,128]{1,0:T(8,128)S(1)}, f32[776,128]{1,0:T(8,128)S(1)}, u32[]{:S(2)}, u32[]{:S(2)}) collective-permute-start(f32[776,128]{1,0:T(8,128)S(1)} %slice.29), channel_id=1, source_target_pairs={{32,2},{33,3},{34,4},{35,5},{36,6},{37,7},{38,8},{39,9},{40,10},{4... | collective-permute-start | bytes 1191944 | tf_op jit(solution)/shard_map/ppermute | solution.py:251
  22.5 0.1 collective-permute-start.5
  22.6 11.7 %collective-permute-done.5 = f32[392,128]{1,0:T(8,128)S(1)} collective-permute-done((f32[392,128]{1,0:T(8,128)S(1)}, f32[392,128]{1,0:T(8,128)S(1)}, u32[]{:S(2)}, u32[]{:S(2)}) %collective-permute-start.5) | collective-permute-done | bytes 200736 | tf_op jit(solution)/shard_map/ppermute | solution.py:252
  34.3 0.0 collective-permute-done.3
  34.3 0.0 collective-permute-done.4
  34.3 0.0 collective-permute-done.2
  34.3 0.1 pad_add_fusion
  34.5 1.6 %collective-permute-start.6 = (f32[520,128]{1,0:T(8,128)S(1)}, f32[520,128]{1,0:T(8,128)S(1)}, u32[]{:S(2)}, u32[]{:S(2)}) collective-permute-start(f32[520,128]{1,0:T(8,128)S(1)} %get-tuple-element.17), channel_id=1, source_target_pairs={{0,32},{1,33},{2,34},{3,35},{4,36},{5,37},{6,38},{7,39},{8,40},{9,... | collective-permute-start | bytes 798728 | tf_op jit(solution)/shard_map/ppermute | solution.py:202
  36.1 1.2 %collective-permute-done.6.b_ref = f32[520,128]{1,0:T(8,128)S(1)} collective-permute-done((f32[520,128]{1,0:T(8,128)S(1)}, f32[520,128]{1,0:T(8,128)S(1)}, u32[]{:S(2)}, u32[]{:S(2)}) %collective-permute-start.6) | collective-permute-done | bytes 266272 | tf_op jit(solution)/shard_map/ppermute | solution.py:202
  37.3 0.9 %last.1 = f32[256,256]{1,0:T(8,128)} custom-call(f32[520,128]{1,0:T(8,128)S(1)} %get-tuple-element.18.a_ref, f32[520,128]{1,0:T(8,128)S(1)} %collective-permute-done.6.b_ref), custom_call_target="tpu_custom_call" | custom-call | tf_op jit(solution)/shard_map/last/pallas_call | solution.py:260
  (5 shorter events, 0.2 us)
Async XLA Ops:
  6.4 4.8 %collective-permute-start = (f32[904,128]{1,0:T(8,128)S(1)}, f32[904,128]{1,0:T(8,128)S(1)}, u32[]{:S(2)}, u32[]{:S(2)}) collective-permute-start(f32[904,128]{1,0:T(8,128)S(1)} %get-tuple-element.14), channel_id=1, source_target_pairs={{0,32},{1,33},{2,34},{3,35},{4,36},{5,37},{6,38},{7,39},{8,40},{9,... | collective-permute-start | bytes 1388552 | tf_op jit(solution)/shard_map/ppermute | solution.py:202
  9.7 4.8 %collective-permute-start.1 = (f32[1296,128]{1,0:T(8,128)S(1)}, f32[1296,128]{1,0:T(8,128)S(1)}, u32[]{:S(2)}, u32[]{:S(2)}) collective-permute-start(f32[1296,128]{1,0:T(8,128)S(1)} %get-tuple-element.16), channel_id=1, source_target_pairs={{0,32},{1,33},{2,34},{3,35},{4,36},{5,37},{6,38},{7,39},{8,40},{9,... | collective-permute-start | bytes 1990664 | tf_op jit(solution)/shard_map/ppermute | solution.py:202
  11.2 23.0 %collective-permute-start.3 = (f32[904,128]{1,0:T(8,128)S(1)}, f32[904,128]{1,0:T(8,128)S(1)}, u32[]{:S(2)}, u32[]{:S(2)}) collective-permute-start(f32[904,128]{1,0:T(8,128)S(1)} %merge.1), channel_id=1, source_target_pairs={{64,32},{65,33},{66,34},{67,35},{68,36},{69,37},{70,38},{71,39},{7... | collective-permute-start | bytes 1388552 | tf_op jit(solution)/shard_map/ppermute | solution.py:248
  14.7 19.6 %collective-permute-start.2 = (f32[904,128]{1,0:T(8,128)S(1)}, f32[904,128]{1,0:T(8,128)S(1)}, u32[]{:S(2)}, u32[]{:S(2)}) collective-permute-start(f32[904,128]{1,0:T(8,128)S(1)} %slice_add_fusion), channel_id=1, source_target_pairs={{0,33},{1,34},{2,35},{3,36},{4,37},{5,38},{6,39},{7,40},{8,41},{9,... | collective-permute-start | bytes 1388552 | tf_op jit(solution)/shard_map/ppermute | solution.py:250
  16.0 18.3 %collective-permute-start.4 = (f32[776,128]{1,0:T(8,128)S(1)}, f32[776,128]{1,0:T(8,128)S(1)}, u32[]{:S(2)}, u32[]{:S(2)}) collective-permute-start(f32[776,128]{1,0:T(8,128)S(1)} %slice.29), channel_id=1, source_target_pairs={{32,2},{33,3},{34,4},{35,5},{36,6},{37,7},{38,8},{39,9},{40,10},{4... | collective-permute-start | bytes 1191944 | tf_op jit(solution)/shard_map/ppermute | solution.py:251
  22.5 11.8 %collective-permute-start.5 = (f32[392,128]{1,0:T(8,128)S(1)}, f32[392,128]{1,0:T(8,128)S(1)}, u32[]{:S(2)}, u32[]{:S(2)}) collective-permute-start(f32[392,128]{1,0:T(8,128)S(1)} %slice_add_fusion.1), channel_id=1, source_target_pairs={{0,3},{1,4},{2,5},{3,6},{4,7},{5,8},{6,9},{7,10},{8,11},{9,12},{10... | collective-permute-start | bytes 602120 | tf_op jit(solution)/shard_map/ppermute | solution.py:252
  34.5 2.8 %collective-permute-start.6 = (f32[520,128]{1,0:T(8,128)S(1)}, f32[520,128]{1,0:T(8,128)S(1)}, u32[]{:S(2)}, u32[]{:S(2)}) collective-permute-start(f32[520,128]{1,0:T(8,128)S(1)} %get-tuple-element.17), channel_id=1, source_target_pairs={{0,32},{1,33},{2,34},{3,35},{4,36},{5,37},{6,38},{7,39},{8,40},{9,... | collective-permute-start | bytes 798728 | tf_op jit(solution)/shard_map/ppermute | solution.py:202
